TPU v7x, 256 devices: a whole 4x4x8 slice. The times are simulated.
256 devices in a mesh: row: 64 (over z, x, core), col: 4 (over y).
Axes of the slice: x: 4, y: 4, z: 8, core: 2. Of those that a mesh axis runs over, the one named last changes fastest.
Arguments:
- hamiltonian: bfloat16 [18432, 128, 128], P('row'), may hold values from -0.15625 to 0.15625
- block_column: int32 [18432], P('row'), may hold values from 0 to 1535, as said below
- vectors: bfloat16 [196608, 512], P('row', 'col'), may hold values from -6 to 6
Outputs:
- filtered: bfloat16 [196608, 512], P('row', 'col')
- intersection: float32 [512, 512], P('col')
Inputs may be any that keep to these rules, and one draw needn't show every extreme that they name: Block row b's entries are block_column[b * 12 + k]. Entry k = 0 is b itself. Entries k < 10 are distinct and lie among the 24 block rows of b's own index of row (block rows i * 24 to i * 24 + 23 for i = b // 24). For k >= 10, let s = (b % 24) * 2 + k - 10 and g = s // 12; the entry lies among the block rows of index (i + o) mod 64, with o = g + 1 if g < 2, else 2 - 1 - g.
All inputs are finite; a program needn't handle non-finite values.
Results may differ from a plain program's by a relative error of at most 0.0056.
Values may be sent and summed in bfloat16 or wider, within the bound.
A program may use at most 192 MiB of HBM per device.

v0:
```python
import jax
import jax.numpy as jnp
from jax import lax
from jax.sharding import PartitionSpec as P

RPR = 2
REACH = 2
STEPS = 3


filter_center = 0.2
filter_half = 0.8


def from_behind(block, axis, distance):
    devices = range(lax.axis_size(axis))
    route = [((i - distance) % len(devices), i) for i in devices]
    return lax.ppermute(block, axis, route)


def on_device(hamiltonian, block_column, vectors):
    block_size = hamiltonian.shape[1]
    row_count = vectors.shape[0] // block_size
    width_dev = vectors.shape[1]
    per_row = hamiltonian.shape[0] // row_count
    local_count = per_row - RPR
    devices = lax.axis_size("row")
    capacity = RPR * row_count // (2 * REACH)
    offsets = [number + 1 for number in range(REACH)] + [-(number + 1) for number in range(REACH)]
    matrix_rows = hamiltonian.reshape(row_count, per_row, block_size, block_size)
    columns = block_column.reshape(row_count, per_row) % row_count
    local_index = columns[:, :local_count]
    wanted = columns[:, local_count:].reshape(2 * REACH, capacity)
    spread = jnp.arange(2 * REACH * capacity) // capacity * row_count + wanted.reshape(-1)
    remote_index = spread.reshape(row_count, RPR)

    def fetch_remote(blocks):
        stacked = jnp.concatenate(
            [from_behind(blocks, "row", -offset) for offset in offsets], axis=0
        )
        return stacked[remote_index]

    def operate(blocks):
        remote = fetch_remote(blocks)
        gathered = jnp.concatenate([blocks[local_index], remote], axis=1)
        return jnp.einsum(
            "rqij,rqjk->rik", matrix_rows, gathered, preferred_element_type=jnp.float32
        )

    previous = vectors.reshape(row_count, block_size, width_dev)
    current = (
        (operate(previous) - filter_center * previous.astype(jnp.float32)) / filter_half
    ).astype(jnp.bfloat16)
    for section in range(STEPS - 1):
        product = operate(current)
        following = (
            2.0 * (product - filter_center * current.astype(jnp.float32)) / filter_half
            - previous.astype(jnp.float32)
        ).astype(jnp.bfloat16)
        previous, current = (current, following)
    filtered = current.reshape(row_count * block_size, width_dev)
    partial_value = lax.dot_general(
        filtered,
        lax.all_gather(filtered, "col", axis=1, tiled=True),
        (((0,), (0,)), ((), ())),
        preferred_element_type=jnp.float32,
    )
    summed = lax.psum(partial_value, "row")
    return (filtered, summed / (devices * row_count * block_size))


def solution(mesh):
    return jax.shard_map(
        on_device,
        mesh=mesh,
        in_specs=(P("row", None, None), P("row"), P("row", "col")),
        out_specs=(P("row", "col"), P("col", None)),
        check_vma=False,
    )
```

profile of v0, /device:TPU:1, one launch (start us, length us, event | category | flops | bytes accessed | tf_op | source)
XLA Modules:
  0.0 386.9 jit_solution(11213303579981072683)
XLA Ops:
  11.4 4.7 %collective-permute-start.1 = (bf16[24,128,128]{2,1,0:T(8,128)(2,1)}, bf16[24,128,128]{2,1,0:T(8,128)(2,1)S(1)}, u32[]{:S(2)}, u32[]{:S(2)}) collective-permute-start(bf16[24,128,128]{2,1,0:T(8,128)(2,1)} %bitcast.35), channel_id=1, source_target_pairs={{8,0},{12,4},{16,8},{20,12},{24,16},{28,20},{32,24},{36,28},{40,32... | collective-permute-start | bytes 2359304 | tf_op jit(solution)/shard_map/ppermute | solution.py:18
  18.1 9.6 %gather_fusion = bf16[240,128,128]{2,1,0:T(8,128)(2,1)} fusion(bf16[24,128,128]{2,1,0:T(8,128)(2,1)} %bitcast.37, s32[1024]{0:T(1024)S(1)} %pad_clamp_fusion.1), kind=kCustom, calls=%fused_computation | custom fusion | bytes 15729600 | tf_op jit(solution)/shard_map/gather | solution.py:45
  27.7 5.7 %collective-permute-done.3 = bf16[24,128,128]{2,1,0:T(8,128)(2,1)S(1)} collective-permute-done((bf16[24,128,128]{2,1,0:T(8,128)(2,1)}, bf16[24,128,128]{2,1,0:T(8,128)(2,1)S(1)}, u32[]{:S(2)}, u32[]{:S(2)}) %collective-permute-start.3) | collective-permute-done | bytes 786464 | tf_op jit(solution)/shard_map/ppermute | solution.py:18
  35.4 3.9 %collective-permute-done = bf16[24,128,128]{2,1,0:T(8,128)(2,1)S(1)} collective-permute-done((bf16[24,128,128]{2,1,0:T(8,128)(2,1)}, bf16[24,128,128]{2,1,0:T(8,128)(2,1)S(1)}, u32[]{:S(2)}, u32[]{:S(2)}) %collective-permute-start) | collective-permute-done | bytes 786464 | tf_op jit(solution)/shard_map/ppermute | solution.py:18
  41.3 2.8 gather_fusion.1
  44.1 8.5 %fusion.14 = bf16[24,128,128]{2,1,0:T(8,128)(2,1)S(1)} fusion(bf16[24,128,128]{2,1,0:T(8,128)(2,1)S(1)} %bitcast.38, bf16[24,12,128,128]{3,2,1,0:T(8,128)(2,1)} %bitcast.49, bf16[24,2,128,128]{3,2,1,0:T(8,128)(2,1)S(1)} %bitcast.47, bf16[24,10,128,128]{3,2,1,0:T(8,128)(2,1)} %bitcast.41), kind=kOutput, calls=%fused_computation.27 | convolution fusion | flops 1228800000 | bytes 20447232 | tf_op jit(solution)/shard_map/rqij,rqjk->rik/dot_general | solution.py:46
  53.5 7.7 %collective-permute-start.5 = (bf16[24,128,128]{2,1,0:T(8,128)(2,1)S(1)}, bf16[24,128,128]{2,1,0:T(8,128)(2,1)}, u32[]{:S(2)}, u32[]{:S(2)}) collective-permute-start(bf16[24,128,128]{2,1,0:T(8,128)(2,1)S(1)} %fusion.14), channel_id=1, source_target_pairs={{8,0},{12,4},{16,8},{20,12},{24,16},{28,20},{32,24},{36,28},{40,32... | collective-permute-start | bytes 2359304 | tf_op jit(solution)/shard_map/ppermute | solution.py:18
  61.8 8.4 %gather_fusion.2 = bf16[240,128,128]{2,1,0:T(8,128)(2,1)} fusion(bf16[24,128,128]{2,1,0:T(8,128)(2,1)S(1)} %fusion.14, s32[1024]{0:T(1024)S(1)} %pad_clamp_fusion.1), kind=kCustom, calls=%fused_computation.2 | custom fusion | bytes 15729600 | tf_op jit(solution)/shard_map/gather | solution.py:45
  70.2 7.6 %collective-permute-done.7 = bf16[24,128,128]{2,1,0:T(8,128)(2,1)S(1)} collective-permute-done((bf16[24,128,128]{2,1,0:T(8,128)(2,1)S(1)}, bf16[24,128,128]{2,1,0:T(8,128)(2,1)S(1)}, u32[]{:S(2)}, u32[]{:S(2)}) %collective-permute-start.7) | collective-permute-done | bytes 786464 | tf_op jit(solution)/shard_map/ppermute | solution.py:18
  79.0 2.4 collective-permute-done.4
  81.4 3.0 pad_maximum_fusion.1
  84.5 3.9 gather_fusion.3
  88.4 9.0 %fusion.15 = bf16[24,128,128]{2,1,0:T(8,128)(2,1)S(1)} fusion(bf16[24,128,128]{2,1,0:T(8,128)(2,1)S(1)} %bitcast.39, bf16[24,128,128]{2,1,0:T(8,128)(2,1)S(1)} %fusion.14, bf16[24,12,128,128]{3,2,1,0:T(8,128)(2,1)} %bitcast.50, bf16[24,2,128,128]{3,2,1,0:T(8,128)(2,1)} %bitcast.48, bf16[24,10,128,128]{3,2,1,0:T(8,128)(2,1)} %bitcast.42), kind=kOutput, calls=%fused_computation.28 | convolution fusion | flops 1229586432 | bytes 21233664 | tf_op jit(solution)/shard_map/rqij,rqjk->rik/dot_general | solution.py:46
  97.4 3.0 collective-permute-start.11
  100.4 8.1 %collective-permute-start.9 = (bf16[24,128,128]{2,1,0:T(8,128)(2,1)S(1)}, bf16[24,128,128]{2,1,0:T(8,128)(2,1)}, u32[]{:S(2)}, u32[]{:S(2)}) collective-permute-start(bf16[24,128,128]{2,1,0:T(8,128)(2,1)S(1)} %fusion.15), channel_id=1, source_target_pairs={{8,0},{12,4},{16,8},{20,12},{24,16},{28,20},{32,24},{36,28},{40,32... | collective-permute-start | bytes 2359304 | tf_op jit(solution)/shard_map/ppermute | solution.py:18
  109.2 8.4 %gather_fusion.4 = bf16[240,128,128]{2,1,0:T(8,128)(2,1)} fusion(bf16[24,128,128]{2,1,0:T(8,128)(2,1)S(1)} %fusion.15, s32[1024]{0:T(1024)S(1)} %pad_clamp_fusion.1), kind=kCustom, calls=%fused_computation.4 | custom fusion | bytes 15729600 | tf_op jit(solution)/shard_map/gather | solution.py:45
  117.6 8.3 %collective-permute-done.11 = bf16[24,128,128]{2,1,0:T(8,128)(2,1)S(1)} collective-permute-done((bf16[24,128,128]{2,1,0:T(8,128)(2,1)S(1)}, bf16[24,128,128]{2,1,0:T(8,128)(2,1)S(1)}, u32[]{:S(2)}, u32[]{:S(2)}) %collective-permute-start.11) | collective-permute-done | bytes 786464 | tf_op jit(solution)/shard_map/ppermute | solution.py:18
  126.2 2.2 collective-permute-done.8
  128.4 3.0 pad_maximum_fusion.2
  131.4 3.9 gather_fusion.5
  135.3 9.9 %fusion.18 = bf16[24,128,128]{2,1,0:T(8,128)(2,1)} fusion(bf16[24,128,128]{2,1,0:T(8,128)(2,1)S(1)} %fusion.14, bf16[24,128,128]{2,1,0:T(8,128)(2,1)S(1)} %fusion.15, bf16[24,12,128,128]{3,2,1,0:T(8,128)(2,1)} %bitcast.51, bf16[24,2,128,128]{3,2,1,0:T(8,128)(2,1)} %bitcast.46, bf16[24,10,128,128]{3,2,1,0:T(8,128)(2,1)} %bitcast.40), kind=kOutput, calls=%fused_computation.31 | convolution fusion | flops 1229586432 | bytes 21233664 | tf_op jit(solution)/shard_map/rqij,rqjk->rik/dot_general | solution.py:46
  145.2 52.0 %all-gather.2.cloned.1.call-done = bf16[3072,512]{1,0:T(8,128)(2,1)} async-done(((bf16[3072,128]{1,0:T(8,128)(2,1)}), bf16[3072,512]{1,0:T(8,128)(2,1)}) %all-gather.2.cloned.1.call-update) | async-done | bytes 3145744 | tf_op jit(solution)/shard_map/all_gather | solution.py:64
  197.2 3.5 fusion.32
  200.7 177.7 %all-reduce.2.cloned.1.call-done = f32[128,512]{1,0:T(8,128)} async-done(((f32[128,512]{1,0:T(8,128)}), f32[128,512]{1,0:T(8,128)}) %all-reduce.2.cloned.1.call-update) | async-done | bytes 262160 | tf_op jit(solution)/shard_map/psum | solution.py:68
  (31 shorter events, 15.6 us)
Async XLA Ops:
  7.2 190.0 %all-gather.2.cloned.1.call-start = ((), (), s32[]{:S(2)}) async-start(), calls=%async_computation | async-start | bytes 3932160 | tf_op jit(solution)/shard_map/all_gather | solution.py:64
  7.2 26.2 %collective-permute-start.3 = (bf16[24,128,128]{2,1,0:T(8,128)(2,1)}, bf16[24,128,128]{2,1,0:T(8,128)(2,1)S(1)}, u32[]{:S(2)}, u32[]{:S(2)}) collective-permute-start(bf16[24,128,128]{2,1,0:T(8,128)(2,1)} %bitcast.33), channel_id=1, source_target_pairs={{248,0},{252,4},{0,8},{4,12},{8,16},{12,20},{16,24},{20,28},{24,32... | collective-permute-start | bytes 2359304 | tf_op jit(solution)/shard_map/ppermute | solution.py:18
  9.3 26.1 %collective-permute-start.2 = (bf16[24,128,128]{2,1,0:T(8,128)(2,1)}, bf16[24,128,128]{2,1,0:T(8,128)(2,1)S(1)}, u32[]{:S(2)}, u32[]{:S(2)}) collective-permute-start(bf16[24,128,128]{2,1,0:T(8,128)(2,1)} %bitcast.34), channel_id=1, source_target_pairs={{252,0},{0,4},{4,8},{8,12},{12,16},{16,20},{20,24},{24,28},{28,32}... | collective-permute-start | bytes 2359304 | tf_op jit(solution)/shard_map/ppermute | solution.py:18
  11.4 24.1 %collective-permute-start.1 = (bf16[24,128,128]{2,1,0:T(8,128)(2,1)}, bf16[24,128,128]{2,1,0:T(8,128)(2,1)S(1)}, u32[]{:S(2)}, u32[]{:S(2)}) collective-permute-start(bf16[24,128,128]{2,1,0:T(8,128)(2,1)} %bitcast.35), channel_id=1, source_target_pairs={{8,0},{12,4},{16,8},{20,12},{24,16},{28,20},{32,24},{36,28},{40,32... | collective-permute-start | bytes 2359304 | tf_op jit(solution)/shard_map/ppermute | solution.py:18
  16.1 23.3 %collective-permute-start = (bf16[24,128,128]{2,1,0:T(8,128)(2,1)}, bf16[24,128,128]{2,1,0:T(8,128)(2,1)S(1)}, u32[]{:S(2)}, u32[]{:S(2)}) collective-permute-start(bf16[24,128,128]{2,1,0:T(8,128)(2,1)} %bitcast.36), channel_id=1, source_target_pairs={{4,0},{8,4},{12,8},{16,12},{20,16},{24,20},{28,24},{32,28},{36,32}... | collective-permute-start | bytes 2359304 | tf_op jit(solution)/shard_map/ppermute | solution.py:18
  41.3 2.8 copy-start
  52.7 25.1 %collective-permute-start.7 = (bf16[24,128,128]{2,1,0:T(8,128)(2,1)S(1)}, bf16[24,128,128]{2,1,0:T(8,128)(2,1)S(1)}, u32[]{:S(2)}, u32[]{:S(2)}) collective-permute-start(bf16[24,128,128]{2,1,0:T(8,128)(2,1)S(1)} %fusion.14), channel_id=1, source_target_pairs={{248,0},{252,4},{0,8},{4,12},{8,16},{12,20},{16,24},{20,28},{24,32... | collective-permute-start | bytes 2359304 | tf_op jit(solution)/shard_map/ppermute | solution.py:18
  53.2 25.8 %collective-permute-start.6 = (bf16[24,128,128]{2,1,0:T(8,128)(2,1)S(1)}, bf16[24,128,128]{2,1,0:T(8,128)(2,1)S(1)}, u32[]{:S(2)}, u32[]{:S(2)}) collective-permute-start(bf16[24,128,128]{2,1,0:T(8,128)(2,1)S(1)} %fusion.14), channel_id=1, source_target_pairs={{252,0},{0,4},{4,8},{8,12},{12,16},{16,20},{20,24},{24,28},{28,32}... | collective-permute-start | bytes 2359304 | tf_op jit(solution)/shard_map/ppermute | solution.py:18
  53.5 25.6 %collective-permute-start.5 = (bf16[24,128,128]{2,1,0:T(8,128)(2,1)S(1)}, bf16[24,128,128]{2,1,0:T(8,128)(2,1)}, u32[]{:S(2)}, u32[]{:S(2)}) collective-permute-start(bf16[24,128,128]{2,1,0:T(8,128)(2,1)S(1)} %fusion.14), channel_id=1, source_target_pairs={{8,0},{12,4},{16,8},{20,12},{24,16},{28,20},{32,24},{36,28},{40,32... | collective-permute-start | bytes 2359304 | tf_op jit(solution)/shard_map/ppermute | solution.py:18
  61.2 20.3 %collective-permute-start.4 = (bf16[24,128,128]{2,1,0:T(8,128)(2,1)S(1)}, bf16[24,128,128]{2,1,0:T(8,128)(2,1)}, u32[]{:S(2)}, u32[]{:S(2)}) collective-permute-start(bf16[24,128,128]{2,1,0:T(8,128)(2,1)S(1)} %fusion.14), channel_id=1, source_target_pairs={{4,0},{8,4},{12,8},{16,12},{20,16},{24,20},{28,24},{32,28},{36,32}... | collective-permute-start | bytes 2359304 | tf_op jit(solution)/shard_map/ppermute | solution.py:18
  97.4 28.5 %collective-permute-start.11 = (bf16[24,128,128]{2,1,0:T(8,128)(2,1)S(1)}, bf16[24,128,128]{2,1,0:T(8,128)(2,1)S(1)}, u32[]{:S(2)}, u32[]{:S(2)}) collective-permute-start(bf16[24,128,128]{2,1,0:T(8,128)(2,1)S(1)} %fusion.15), channel_id=1, source_target_pairs={{248,0},{252,4},{0,8},{4,12},{8,16},{12,20},{16,24},{20,28},{24,32... | collective-permute-start | bytes 2359304 | tf_op jit(solution)/shard_map/ppermute | solution.py:18
  100.4 25.8 %collective-permute-start.10 = (bf16[24,128,128]{2,1,0:T(8,128)(2,1)S(1)}, bf16[24,128,128]{2,1,0:T(8,128)(2,1)S(1)}, u32[]{:S(2)}, u32[]{:S(2)}) collective-permute-start(bf16[24,128,128]{2,1,0:T(8,128)(2,1)S(1)} %fusion.15), channel_id=1, source_target_pairs={{252,0},{0,4},{4,8},{8,12},{12,16},{16,20},{20,24},{24,28},{28,32}... | collective-permute-start | bytes 2359304 | tf_op jit(solution)/shard_map/ppermute | solution.py:18
  100.4 25.8 %collective-permute-start.9 = (bf16[24,128,128]{2,1,0:T(8,128)(2,1)S(1)}, bf16[24,128,128]{2,1,0:T(8,128)(2,1)}, u32[]{:S(2)}, u32[]{:S(2)}) collective-permute-start(bf16[24,128,128]{2,1,0:T(8,128)(2,1)S(1)} %fusion.15), channel_id=1, source_target_pairs={{8,0},{12,4},{16,8},{20,12},{24,16},{28,20},{32,24},{36,28},{40,32... | collective-permute-start | bytes 2359304 | tf_op jit(solution)/shard_map/ppermute | solution.py:18
  108.5 19.9 %collective-permute-start.8 = (bf16[24,128,128]{2,1,0:T(8,128)(2,1)S(1)}, bf16[24,128,128]{2,1,0:T(8,128)(2,1)}, u32[]{:S(2)}, u32[]{:S(2)}) collective-permute-start(bf16[24,128,128]{2,1,0:T(8,128)(2,1)S(1)} %fusion.15), channel_id=1, source_target_pairs={{4,0},{8,4},{12,8},{16,12},{20,16},{24,20},{28,24},{32,28},{36,32}... | collective-permute-start | bytes 2359304 | tf_op jit(solution)/shard_map/ppermute | solution.py:18
  145.2 233.2 %all-reduce.2.cloned.1.call-start = ((), (), s32[]{:S(2)}) async-start(), calls=%async_computation.1 | async-start | bytes 524288 | tf_op jit(solution)/shard_map/psum | solution.py:68
Sparse Core Ops, SparseCore 0:
  145.3 51.8 all-gather.1
  201.3 177.0 all-reduce.1
where the time goes:
time: 387 us
  waiting for transfers between devices  263 us (68%)
  local copies, waits for them, and re-layouts  37.2 us (10%)
  matrix products  30.9 us (8%)
  starting transfers between devices  30.8 us (8%)
  between operations  14.1 us (4%)
  other arithmetic  10.5 us (3%)
    psum x1, waiting for transfers between devices, on_device(): summed = lax.psum(partial_value, 'row')  178 us
    all_gather x1, waiting for transfers between devices, on_device(): lax.all_gather(filtered, 'col', axis=1, tiled=True)  52 us
    ppermute x12, waiting for transfers between devices, from_behind(): return lax.ppermute(block, axis, route)  33.7 us
    ppermute x12, starting transfers between devices, from_behind(): return lax.ppermute(block, axis, route)  30.7 us
    dot_general x3, matrix products, operate(): jnp.einsum('rqij,rqjk->rik', matrix_rows, gathered, preferred_element_typ...  27.4 us
    gather x3, local copies, waits for them, and re-layouts, operate(): gathered = jnp.concatenate([blocks[local_index], remote], axis=1)  26.4 us
    gather x3, local copies, waits for them, and re-layouts, fetch_remote(): return stacked[remote_index]  10.5 us
    concatenate x3, other arithmetic, fetch_remote(): jnp.concatenate([from_behind(blocks, 'row', -offset) for offset in offset...  8.01 us
  transfers between devices with their start and end apart: 14, of which 11 were waited for; matrix products, arithmetic and copies ran while one was open for 7% of the time, Pallas kernels for 0%

commit v1 on v0

v1 whole, which is shorter than its diff:
```python
import functools

import jax
import jax.numpy as jnp
from jax import lax
from jax.experimental import pallas as pl
from jax.experimental.pallas import tpu as pltpu
from jax.sharding import PartitionSpec as P

MESH = pl.DeviceIdType.MESH
STEPS = 3
OFFSETS = (1, 2, -1, -2)
ORDER = (1, 3, 0, 2)
BF16 = jnp.bfloat16
F32 = jnp.float32
CENTER = 0.2
HALF = 0.8
X = 4
Y = 4


def kernel(
    rows,
    norb,
    bc_s,
    bc_h,
    h_hbm,
    v_hbm,
    f_hbm,
    inter,
    ham,
    vec,
    acc,
    hrem,
    psend,
    precv,
    ridx,
    mine,
    half_recv,
    tsum,
    y_recv,
    usum,
    x_recv,
    zsum,
    z_recv,
    final,
    every,
    ssum,
    load_sem,
    idx_sem,
    h_sem,
    fwd_sem,
    p_sem,
    a_sem,
    s_sem,
    out_sem,
):
    z_count = rows // (2 * X)
    r = lax.axis_index("row")
    y = lax.axis_index("col")
    core = lax.rem(r, 2)
    x = lax.rem(r // 2, X)
    z = r // (2 * X)
    bs = ham.shape[-1]
    quarter, eighth = bs // 4, bs // 8
    base = r * 24

    def inside(entry):
        return jnp.clip(entry - base, 0, 23)

    def row_at(offset):
        return lax.rem(r + offset + rows, rows)

    def col_at(offset):
        return lax.rem(y + offset + Y, Y)

    def x_at(offset, c):
        return z * 2 * X + lax.rem(x + offset, X) * 2 + c

    def z_at(offset):
        return lax.rem(z + offset, z_count) * 2 * X + x * 2 + core

    loads = [pltpu.make_async_copy(v_hbm, vec.at[0], load_sem.at[4])]
    loads += [
        pltpu.make_async_copy(
            h_hbm.at[pl.ds(6 * g, 6)], ham.at[pl.ds(6 * g, 6)], load_sem.at[g]
        )
        for g in range(4)
    ]
    for load in loads:
        load.start()

    peers = [(row_at(o), y) for o in OFFSETS]
    peers += [(r, col_at(d)) for d in range(1, Y)]
    peers += [(x_at(d, c), y) for d in range(1, X) for c in range(2)]
    peers += [(z_at(d), y) for d in range(1, z_count)]
    barrier = pltpu.get_barrier_semaphore()
    for peer in peers:
        pl.semaphore_signal(barrier, inc=1, device_id=peer, device_id_type=MESH)
    pl.semaphore_wait(barrier, len(peers))

    def remote(src, dst, send, recv, peer):
        return pltpu.make_async_remote_copy(
            src_ref=src,
            dst_ref=dst,
            send_sem=send,
            recv_sem=recv,
            device_id=peer,
            device_id_type=MESH,
        )

    g_x_out, g_chip_out = 2 * (1 - core), 2 * core
    g_x_in, g_chip_in = 2 * core, 2 * (1 - core)
    to_row = (row_at(2), row_at(-2), lax.rem(r + 2 * core - 1 + rows, rows))
    partner = r + 1 - 2 * core
    out_group = (1, 3, g_x_out)
    in_group = (1, 3, g_x_in)

    def rows_of(part, size):
        return pl.ds(pl.multiple_of(part * size, size), size)

    h_copies = []
    for j in range(3):
        g = out_group[j]
        copy = remote(
            h_hbm.at[pl.ds(6 * g, 6), pl.ds(10, 2), rows_of(y, quarter)],
            hrem.at[g, :, :, rows_of(y, quarter)],
            h_sem.at[0, j],
            h_sem.at[1, j],
            (to_row[j], y),
        )
        copy.start()
        h_copies.append(copy)
    idx_copies = []
    for g in range(4):
        copy = remote(
            bc_h, ridx.at[g], idx_sem.at[0, g], idx_sem.at[1, g], (row_at(OFFSETS[g]), y)
        )
        copy.start()
        idx_copies.append(copy)
    chip_copy = remote(
        h_hbm.at[pl.ds(6 * g_chip_out, 6), pl.ds(10, 2)],
        hrem.at[g_chip_out],
        h_sem.at[0, 3],
        h_sem.at[1, 3],
        (partner, y),
    )
    chip_copy.start()

    def local_rows(current, first_row, count):
        def body(i, carry):
            b = first_row + i
            lhs = jnp.concatenate([ham[b, k] for k in range(10)], axis=1)
            rhs = jnp.concatenate(
                [vec[current, inside(bc_s[b * 12 + k])] for k in range(10)], axis=0
            )
            acc[b] = jnp.dot(lhs, rhs, preferred_element_type=F32)
            return carry

        lax.fori_loop(0, count, body, 0, unroll=2)

    def products(step, g):
        def body(i, carry):
            lhs = jnp.concatenate([hrem[g, i, 0], hrem[g, i, 1]], axis=1)
            rhs = jnp.concatenate(
                [
                    vec[step, inside(ridx[g, (6 * g + i) * 12 + 10 + q])]
                    for q in range(2)
                ],
                axis=0,
            )
            psend[step, g, i] = jnp.dot(lhs, rhs, preferred_element_type=F32).astype(BF16)
            return carry

        lax.fori_loop(0, 6, body, 0, unroll=2)

    def send_products(step, g):
        copy = remote(
            psend.at[step, g],
            precv.at[step, g],
            p_sem.at[0, step, g],
            p_sem.at[1, step, g],
            (row_at(-OFFSETS[g]), y),
        )
        copy.start()
        return copy

    loads[0].wait()
    loads[1].wait()
    local_rows(0, 0, 6)

    fwd = []
    for j in range(3):
        h_copies[j].wait_recv()
        part = hrem.at[in_group[j], :, :, rows_of(y, quarter)]
        pair = []
        for side, d in enumerate((1, -1)):
            copy = remote(
                part, part, fwd_sem.at[0, j, side], fwd_sem.at[1, j, side], (r, col_at(d))
            )
            copy.start()
            pair.append(copy)
        fwd.append(pair)

    loads[2].wait()
    local_rows(0, 6, 6)

    second = []
    for j in range(3):
        pair = []
        for side, d in enumerate((1, -1)):
            fwd[j][side].wait_recv()
            part = hrem.at[
                in_group[j], :, :, rows_of(col_at(-d) * 2 + side, eighth)
            ]
            copy = remote(
                part, part, fwd_sem.at[0, j, 2 + side], fwd_sem.at[1, j, 2 + side], (r, col_at(d))
            )
            copy.start()
            pair.append(copy)
        second.append(pair)

    loads[3].wait()
    local_rows(0, 12, 6)
    loads[4].wait()
    local_rows(0, 18, 6)

    for copy in idx_copies:
        copy.wait_recv()

    p_copies = []

    def finish(step, g, copy):
        copy.wait_recv()

        def body(i, carry):
            b = 6 * g + i
            product = acc[b] + precv[step, g, i].astype(F32)
            shifted = product - CENTER * vec[step, b].astype(F32)
            if step == 0:
                vec[1, b] = (shifted / HALF).astype(BF16)
            else:
                vec[step + 1, b] = (
                    2.0 * shifted / HALF - vec[step - 1, b].astype(F32)
                ).astype(BF16)
            return carry

        lax.fori_loop(0, 6, body, 0, unroll=2)

    def receive(step, g):
        return remote(
            psend.at[step, g], precv.at[step, g], p_sem.at[0, step, g], p_sem.at[1, step, g], (r, y)
        )

    arrival = (g_chip_out, 1, 3, g_x_out)
    for step in range(STEPS):
        if step == 0:
            for j in range(3):
                for copy in second[j]:
                    copy.wait_recv()
                g = in_group[j]
                products(0, g)
                o = OFFSETS[g] if j < 2 else 1 - 2 * core
                copy = remote(
                    psend.at[0, g],
                    precv.at[0, g],
                    p_sem.at[0, 0, g],
                    p_sem.at[1, 0, g],
                    (row_at(-o), y),
                )
                copy.start()
                p_copies.append(copy)
            chip_copy.wait_recv()
            products(0, g_chip_in)
            copy = remote(
                psend.at[0, g_chip_in],
                precv.at[0, g_chip_in],
                p_sem.at[0, 0, g_chip_in],
                p_sem.at[1, 0, g_chip_in],
                (partner, y),
            )
            copy.start()
            p_copies.append(copy)
        else:
            for g in ORDER:
                products(step, g)
                p_copies.append(send_products(step, g))
            local_rows(step, 0, 24)
        for g in arrival:
            finish(step, g, receive(step, g))
            if step == STEPS - 1:

                @pl.when(g != y)
                def _():
                    remote(
                        vec.at[STEPS, pl.ds(6 * g, 6)],
                        mine.at[y],
                        a_sem.at[0, g],
                        a_sem.at[1, y],
                        (r, g),
                    ).start()

                @pl.when(g == y)
                def _():
                    pltpu.make_async_copy(
                        vec.at[STEPS, pl.ds(6 * g, 6)], mine.at[y], a_sem.at[1, y]
                    ).start()

                pltpu.make_async_copy(
                    vec.at[STEPS, pl.ds(6 * g, 6)],
                    f_hbm.at[pl.ds(6 * g, 6)],
                    out_sem.at[g],
                ).start()

    pltpu.make_async_copy(
        vec.at[STEPS, pl.ds(6 * y, 6)], mine.at[y], a_sem.at[1, y]
    ).wait()
    for d in range(1, Y):
        s = col_at(d)
        remote(
            vec.at[STEPS, pl.ds(6 * s, 6)], mine.at[s], a_sem.at[0, s], a_sem.at[1, s], (r, s)
        ).wait_recv()

    depth = 6 * bs
    everything = jnp.concatenate(
        [mine[s].reshape(depth, bs) for s in range(Y)], axis=1
    )

    for i in range(Y):
        part = lax.dot_general(
            mine[i].reshape(depth, bs),
            everything,
            (((0,), (0,)), ((), ())),
            preferred_element_type=F32,
        )
        for c in range(2):
            ssum[c, i] = part[:, c * 2 * bs : (c + 1) * 2 * bs].astype(BF16)

    copy_c = remote(
        ssum.at[1 - core], half_recv, s_sem.at[0, 0], s_sem.at[1, 0], (partner, y)
    )
    copy_c.start()
    copy_c.wait_recv()
    for i in range(Y):
        tsum[i] = (ssum[core, i].astype(F32) + half_recv[i].astype(F32)).astype(BF16)

    y_copies = []
    for d in range(1, Y):
        s = col_at(d)
        copy = remote(
            tsum.at[s], y_recv.at[Y - d], s_sem.at[0, d], s_sem.at[1, d], (r, s)
        )
        copy.start()
        y_copies.append(copy)
    total = tsum[y].astype(F32)
    for d in range(1, Y):
        y_copies[d - 1].wait_recv()
    for d in range(1, Y):
        total += y_recv[d].astype(F32)
    for i in range(X):
        usum[i] = total[i * quarter : (i + 1) * quarter].astype(BF16)

    x_copies = []
    for d in range(1, X):
        copy = remote(
            usum.at[lax.rem(x + d, X)],
            x_recv.at[X - d],
            s_sem.at[0, 3 + d],
            s_sem.at[1, 3 + d],
            (x_at(d, core), y),
        )
        copy.start()
        x_copies.append(copy)
    total = usum[x].astype(F32)
    for d in range(1, X):
        x_copies[d - 1].wait_recv()
    for d in range(1, X):
        total += x_recv[d].astype(F32)
    zsum[...] = total.astype(BF16)

    z_copies = []
    for d in range(1, z_count):
        copy = remote(
            zsum,
            z_recv.at[z_count - d],
            s_sem.at[0, 6 + d],
            s_sem.at[1, 6 + d],
            (z_at(d), y),
        )
        copy.start()
        z_copies.append(copy)
    total = zsum[...].astype(F32)
    for copy in z_copies:
        copy.wait_recv()
    for d in range(1, z_count):
        total += z_recv[d].astype(F32)
    final[...] = total / norb

    last = []
    for d in range(X):
        for e in range(2):
            if d == 0 and e == 0:
                continue
            n = 14 + 2 * d + e
            copy = remote(
                final,
                every.at[X - d if d else 0, e],
                s_sem.at[0, n],
                s_sem.at[1, n],
                (x_at(d, lax.rem(core + e, 2)), y),
            )
            copy.start()
            last.append(copy)

    def place(xx, c, value):
        inter[rows_of(xx, quarter), pl.ds(pl.multiple_of(c * 2 * bs, 2 * bs), 2 * bs)] = value

    place(x, core, final[...])
    for copy in last:
        copy.wait_recv()
    for d in range(X):
        for e in range(2):
            if d == 0 and e == 0:
                continue
            place(
                lax.rem(x + (X - d), X),
                lax.rem(core + e, 2),
                every[X - d if d else 0, e],
            )

    for group in ([chip_copy], h_copies, idx_copies, p_copies, y_copies, x_copies, z_copies, last, [copy_c]):
        for copy in group:
            copy.wait_send()
    for pair in fwd + second:
        for copy in pair:
            copy.wait_send()
    for d in range(1, Y):
        s = col_at(d)
        remote(
            vec.at[STEPS, pl.ds(6 * s, 6)], mine.at[y], a_sem.at[0, s], a_sem.at[1, y], (r, s)
        ).wait_send()
    for g in range(4):
        pltpu.make_async_copy(
            vec.at[STEPS, pl.ds(6 * g, 6)], f_hbm.at[pl.ds(6 * g, 6)], out_sem.at[g]
        ).wait()


def on_device(hamiltonian, block_column, vectors):
    bs = hamiltonian.shape[1]
    rows = lax.axis_size("row")
    z_count = rows // (2 * X)
    ham = hamiltonian.reshape(24, 12, bs, bs)
    vec = vectors.reshape(24, bs, bs)
    dma = pltpu.SemaphoreType.DMA
    any_spec = pl.BlockSpec(memory_space=pl.ANY)
    filtered, inter = pl.pallas_call(
        functools.partial(kernel, rows, float(rows * 24 * bs)),
        out_shape=(
            jax.ShapeDtypeStruct((24, bs, bs), BF16),
            jax.ShapeDtypeStruct((bs, Y * bs), F32),
        ),
        in_specs=[pl.BlockSpec(memory_space=pltpu.SMEM), any_spec, any_spec, any_spec],
        out_specs=(any_spec, pl.BlockSpec(memory_space=pltpu.VMEM)),
        scratch_shapes=[
            pltpu.VMEM((24, 12, bs, bs), BF16),
            pltpu.VMEM((STEPS + 1, 24, bs, bs), BF16),
            pltpu.VMEM((24, bs, bs), F32),
            pltpu.VMEM((4, 6, 2, bs, bs), BF16),
            pltpu.VMEM((STEPS, 4, 6, bs, bs), BF16),
            pltpu.VMEM((STEPS, 4, 6, bs, bs), BF16),
            pltpu.SMEM((4, 288), jnp.int32),
            pltpu.VMEM((Y, 6, bs, bs), BF16),
            pltpu.VMEM((Y, bs, 2 * bs), BF16),
            pltpu.VMEM((Y, bs, 2 * bs), BF16),
            pltpu.VMEM((Y, bs, 2 * bs), BF16),
            pltpu.VMEM((X, bs // 4, 2 * bs), BF16),
            pltpu.VMEM((X, bs // 4, 2 * bs), BF16),
            pltpu.VMEM((bs // 4, 2 * bs), BF16),
            pltpu.VMEM((z_count, bs // 4, 2 * bs), BF16),
            pltpu.VMEM((bs // 4, 2 * bs), F32),
            pltpu.VMEM((X, 2, bs // 4, 2 * bs), F32),
            pltpu.VMEM((2, Y, bs, 2 * bs), BF16),
            dma((5,)),
            dma((2, 4)),
            dma((2, 4)),
            dma((2, 3, 4)),
            dma((2, STEPS, 4)),
            dma((2, 4)),
            dma((2, 22)),
            dma((4,)),
        ],
        compiler_params=pltpu.CompilerParams(
            collective_id=0, has_side_effects=True, vmem_limit_bytes=50 * 2**20
        ),
        name="chebyshev",
    )(block_column, block_column, ham, vec)
    return filtered.reshape(24 * bs, bs), inter


def solution(mesh):
    return jax.shard_map(
        on_device,
        mesh=mesh,
        in_specs=(P("row", None, None), P("row"), P("row", "col")),
        out_specs=(P("row", "col"), P("col", None)),
        check_vma=False,
    )
```

time: 387 us -> 89 us (0.23)
  waiting for transfers between devices: 263 us -> 0 us
  Pallas kernels: 0 us -> 84.8 us
  local copies, waits for them, and re-layouts: 37.2 us -> 3.39 us
  matrix products: 30.9 us -> 0 us
  starting transfers between devices: 30.8 us -> 0 us
  between operations: 14.1 us -> 0.65 us
  other arithmetic: 10.5 us -> 0 us
    psum x1 -> x0, waiting for transfers between devices: 178 us -> none  [on_device(): summed = lax.psum(partial_value, 'row')]
    pallas_call x0 -> x1, Pallas kernels: none -> 84.8 us  [on_device(): pl.pallas_call(functools.partial(kernel, rows, float(rows * 24 * bs)), ou...]
    all_gather x1 -> x0, waiting for transfers between devices: 52 us -> none  [on_device(): lax.all_gather(filtered, 'col', axis=1, tiled=True)]
    gather x6 -> x0, local copies, waits for them, and re-layouts: 36.9 us -> none  [the longest x3 26.4 us: operate(): gathered = jnp.concatenate([blocks[local_index], remote], axis=1)]
    ppermute x12 -> x0, waiting for transfers between devices: 33.7 us -> none  [from_behind(): return lax.ppermute(block, axis, route)]
    dot_general x4 -> x0, matrix products: 30.9 us -> none  [the longest x3 27.4 us: operate(): jnp.einsum('rqij,rqjk->rik', matrix_rows, gathered, preferred_element_typ...]
    ppermute x12 -> x0, starting transfers between devices: 30.7 us -> none  [from_behind(): return lax.ppermute(block, axis, route)]
    concatenate x3 -> x0, other arithmetic: 8.01 us -> none  [fetch_remote(): jnp.concatenate([from_behind(blocks, 'row', -offset) for offset in offset...]
  transfers between devices with their start and end apart: 14 -> 0, of which waited for: 11 -> 0; matrix products, arithmetic and copies ran while one was open for 7% -> 0% of each run, Pallas kernels for 0% -> 0%
where the time goes in v1:
time: 89 us; the launch traced here: 88.8 us
  Pallas kernels  84.8 us (95%)
  local copies, waits for them, and re-layouts  3.39 us (4%)
    pallas_call x1, Pallas kernels, on_device(): pl.pallas_call(functools.partial(kernel, rows, float(rows * 24 * bs)), ou...  84.8 us
    unnamed x6, local copies, waits for them, and re-layouts  3.39 us

profile of v1, /device:TPU:1, one launch (start us, length us, event | category | flops | bytes accessed | tf_op | source)
XLA Modules:
  0.0 88.8 jit_solution(7499396647318341412)
XLA Ops:
  0.6 0.0 copy-start
  0.6 1.1 %copy-done = bf16[3072,128]{1,0:T(8,128)(2,1)S(1)} copy-done((bf16[3072,128]{1,0:T(8,128)(2,1)S(1)}, bf16[3072,128]{1,0:T(8,128)(2,1)}, u32[]{:S(2)}) %copy-start) | copy-done | bytes 786456
  1.8 0.0 copy-start.1
  1.8 0.7 copy-done.1
  2.4 84.8 %chebyshev.1 = (bf16[24,128,128]{2,1,0:T(8,128)(2,1)S(1)}, f32[128,512]{1,0:T(8,128)S(1)}) custom-call(s32[288]{0:T(512)S(1)} %copy-done.1, s32[288]{0:T(512)S(1)} %copy-done.1, bf16[24,12,128,128]{3,2,1,0:T(8,128)(2,1)} %bitcast.5, bf16[24,128,128]{2,1,0:T(8,128)(2,1)S(1)} %bitcast.3), custom_call_target="tpu_custom_call" | custom-call | tf_op jit(solution)/shard_map/chebyshev/pallas_call | solution.py:456
  87.3 0.9 copy.7
  88.1 0.7 copy.8
Async XLA Ops:
  0.6 1.1 %copy-start = (bf16[3072,128]{1,0:T(8,128)(2,1)S(1)}, bf16[3072,128]{1,0:T(8,128)(2,1)}, u32[]{:S(2)}) copy-start(bf16[3072,128]{1,0:T(8,128)(2,1)} %param.5) | copy-start | bytes 2359300
  1.8 0.7 copy-start.1

commit v2 on v0

v2 whole, which is shorter than its diff:
```python
import functools

import jax
import jax.numpy as jnp
from jax import lax
from jax.experimental import pallas as pl
from jax.experimental.pallas import tpu as pltpu
from jax.sharding import PartitionSpec as P

MESH = pl.DeviceIdType.MESH
STEPS = 3
OFFSETS = (1, 2, -1, -2)
BF16 = jnp.bfloat16
F32 = jnp.float32
CENTER = 0.2
HALF = 0.8
X = 4
Y = 4
PARTS = 3
PER_PART = 6 // PARTS


def kernel(
    rows,
    norb,
    bc_s,
    bc_h,
    h_hbm,
    v_hbm,
    f_hbm,
    inter,
    ham,
    vec,
    acc,
    hrem,
    psend,
    precv,
    ridx,
    mine,
    half_recv,
    tsum,
    y_recv,
    usum,
    x_recv,
    zsum,
    z_recv,
    final,
    every,
    ssum,
    load_sem,
    idx_sem,
    h_sem,
    fwd_sem,
    p_sem,
    a_sem,
    s_sem,
    out_sem,
):
    z_count = rows // (2 * X)
    r = lax.axis_index("row")
    y = lax.axis_index("col")
    core = lax.rem(r, 2)
    x = lax.rem(r // 2, X)
    z = r // (2 * X)
    bs = ham.shape[-1]
    piece = bs // (2 * X)
    base = r * 24

    def inside(entry):
        return jnp.clip(entry - base, 0, 23)

    def row_at(offset):
        return lax.rem(r + offset + rows, rows)

    def col_at(offset):
        return lax.rem(y + offset + Y, Y)

    def x_at(offset, c):
        return z * 2 * X + lax.rem(x + offset, X) * 2 + c

    def z_at(offset):
        return lax.rem(z + offset, z_count) * 2 * X + x * 2 + core

    sends = []
    loads = {}

    def load(name, src, dst, sem):
        loads[name] = pltpu.make_async_copy(src, dst, sem)
        loads[name].start()

    def loaded(name):
        loads.pop(name).wait()

    def remote(src, dst, send_sem, recv_sem, peer):
        return pltpu.make_async_remote_copy(
            src_ref=src,
            dst_ref=dst,
            send_sem=send_sem,
            recv_sem=recv_sem,
            device_id=peer,
            device_id_type=MESH,
        )

    def send(*args):
        copy = remote(*args)
        copy.start()
        sends.append(copy)
        return copy

    def close():
        for copy in sends:
            copy.wait_send()
        for name in tuple(loads):
            loaded(name)

    load("vec", v_hbm, vec.at[0], load_sem.at[4])

    def load_rows(g):
        load(g, h_hbm.at[pl.ds(6 * g, 6)], ham.at[pl.ds(6 * g, 6)], load_sem.at[g])

    load_rows(0)

    peers = [(row_at(o), y) for o in OFFSETS]
    peers += [(r, col_at(d)) for d in range(1, Y)]
    peers += [(x_at(d, c), y) for d in range(1, X) for c in range(2)]
    peers += [(z_at(d), y) for d in range(1, z_count)]
    barrier = pltpu.get_barrier_semaphore()
    for peer in peers:
        pl.semaphore_signal(barrier, inc=1, device_id=peer, device_id_type=MESH)
    pl.semaphore_wait(barrier, len(peers))

    g_x_out, g_chip_out = 2 * (1 - core), 2 * core
    g_x_in, g_chip_in = 2 * core, 2 * (1 - core)
    to_row = (row_at(2), row_at(-2), lax.rem(r + 2 * core - 1 + rows, rows))
    partner = r + 1 - 2 * core
    out_group = (1, 3, g_x_out)
    in_group = (1, 3, g_x_in)

    def coupled_hbm(g, first, count):
        return h_hbm.at[pl.ds(6 * g + first, count), pl.ds(10, 2)]

    quarter_copies = [
        send(
            coupled_hbm(g, y, 1),
            hrem.at[g, pl.ds(y, 1)],
            h_sem.at[0, j],
            h_sem.at[1, j],
            (to_row[j], y),
        )
        for j, g in enumerate(out_group)
    ]
    chip_copy = send(
        h_hbm.at[pl.ds(6 * g_chip_out, 6), pl.ds(10, 2)],
        hrem.at[g_chip_out],
        h_sem.at[0, 3],
        h_sem.at[1, 3],
        (partner, y),
    )
    idx_copies = [
        send(bc_h, ridx.at[g], idx_sem.at[0, g], idx_sem.at[1, g], (row_at(OFFSETS[g]), y))
        for g in range(4)
    ]
    lower_copies = [
        send(
            coupled_hbm(g, Y, 2),
            hrem.at[g, pl.ds(Y, 2)],
            h_sem.at[0, 4 + j],
            h_sem.at[1, 4 + j],
            (to_row[j], y),
        )
        for j, g in enumerate(out_group)
    ]

    for g in range(1, 4):
        load_rows(g)

    def local_rows(current, first_row, count, unroll):
        def body(i, carry):
            b = first_row + i
            lhs = jnp.concatenate([ham[b, k] for k in range(10)], axis=1)
            rhs = jnp.concatenate(
                [vec[current, inside(bc_s[b * 12 + k])] for k in range(10)], axis=0
            )
            acc[b] = jnp.dot(lhs, rhs, preferred_element_type=F32)
            return carry

        lax.fori_loop(0, count, body, 0, unroll=unroll)

    def products(step, g):
        def body(i, carry):
            lhs = jnp.concatenate([hrem[g, i, 0], hrem[g, i, 1]], axis=1)
            rhs = jnp.concatenate(
                [
                    vec[step, inside(ridx[g, (6 * g + i) * 12 + 10 + q])]
                    for q in range(2)
                ],
                axis=0,
            )
            psend[step, g, i] = jnp.dot(lhs, rhs, preferred_element_type=F32).astype(BF16)
            return carry

        lax.fori_loop(0, 6, body, 0, unroll=6)

    in_groups = (*in_group, g_chip_in)
    back_to = (row_at(-2), row_at(2), lax.rem(r + 2 * core - 1 + rows, rows), partner)

    def product_copy(step, g, h, peer):
        part = pl.ds(PER_PART * h, PER_PART)
        return (
            psend.at[step, g, part],
            precv.at[step, g, part],
            p_sem.at[0, step, h, g],
            p_sem.at[1, step, h, g],
            peer,
        )

    def send_products(step, j, h):
        send(*product_copy(step, in_groups[j], h, (back_to[j], y)))

    loaded("vec")
    loaded(0)
    local_rows(0, 0, 6, 6)

    fwd = []
    for j in range(3):
        quarter_copies[j].wait_recv()
        part = hrem.at[in_group[j], pl.ds(y, 1)]
        fwd.append(
            [
                send(
                    part,
                    part,
                    fwd_sem.at[0, j, side],
                    fwd_sem.at[1, j, side],
                    (r, col_at(d)),
                )
                for side, d in enumerate((1, -1))
            ]
        )

    loaded(1)
    local_rows(0, 6, 6, 6)

    second = []
    for j in range(3):
        pair = []
        for side, d in enumerate((1, -1)):
            fwd[j][side].wait_recv()
            part = hrem.at[in_group[j], pl.ds(col_at(-d), 1), pl.ds(side, 1)]
            pair.append(
                send(
                    part,
                    part,
                    fwd_sem.at[0, j, 2 + side],
                    fwd_sem.at[1, j, 2 + side],
                    (r, col_at(d)),
                )
            )
        second.append(pair)
        if j < 2:
            loaded(2 + j)
            local_rows(0, 12 + 6 * j, 6, 6)

    for copy in idx_copies:
        copy.wait_recv()


    def finish(step, g, h):
        remote(*product_copy(step, g, h, (partner, y))).wait_recv()

        def body(i, carry):
            b = 6 * g + PER_PART * h + i
            product = acc[b] + precv[step, g, PER_PART * h + i].astype(F32)
            shifted = product - CENTER * vec[step, b].astype(F32)
            if step == 0:
                vec[1, b] = (shifted / HALF).astype(BF16)
            else:
                vec[step + 1, b] = (
                    2.0 * shifted / HALF - vec[step - 1, b].astype(F32)
                ).astype(BF16)
            return carry

        lax.fori_loop(0, PER_PART, body, 0, unroll=PER_PART)

    def to_mine(g, h, source=y, local=False):
        group = vec.at[STEPS, pl.ds(6 * g + PER_PART * h, PER_PART)]
        place = mine.at[source, pl.ds(PER_PART * h, PER_PART)]
        if local:
            return pltpu.make_async_copy(group, place, a_sem.at[1, h, y])
        return remote(group, place, a_sem.at[0, h, g], a_sem.at[1, h, source], (r, g))

    def to_hbm(g, h):
        rows_g = pl.ds(6 * g + PER_PART * h, PER_PART)
        return pltpu.make_async_copy(
            vec.at[STEPS, rows_g], f_hbm.at[rows_g], out_sem.at[h, g]
        )

    def scatter(g, h):
        @pl.when(g != y)
        def _():
            to_mine(g, h).start()

        @pl.when(g == y)
        def _():
            to_mine(g, h, local=True).start()

        to_hbm(g, h).start()

    def close_scatter():
        for h in range(PARTS):
            for d in range(1, Y):
                to_mine(col_at(d), h).wait_send()
            for g in range(4):
                to_hbm(g, h).wait()

    own_groups = (1, 3, g_x_out)
    parts = range(PARTS)
    for step in range(STEPS):

        def complete(g, h, step=step):
            finish(step, g, h)
            if step == STEPS - 1:
                scatter(g, h)

        if step == 0:
            for j in range(3):
                for copy in (*second[j], lower_copies[j]):
                    copy.wait_recv()
                products(0, in_groups[j])
                for h in parts:
                    send_products(0, j, h)
            chip_copy.wait_recv()
            products(0, g_chip_in)
            for h in parts:
                send_products(0, 3, h)
        else:
            for j in (0, 1):
                products(step, in_groups[j])
                send_products(step, j, 0)
            products(step, g_chip_in)
            for h in parts:
                send_products(step, 3, h)
            products(step, in_groups[2])
            send_products(step, 2, 0)
            for h in parts[1:]:
                for j in range(3):
                    send_products(step, j, h)
            local_rows(step, 6 * g_chip_out, 6, 6)
        for h in parts:
            complete(g_chip_out, h)
        if step > 0:
            for g in own_groups:
                local_rows(step, 6 * g, 6, 6)
        for h in parts:
            for g in own_groups:
                complete(g, h)

    for h in parts:
        to_mine(y, h, local=True).wait()
        for d in range(1, Y):
            to_mine(col_at(d), h, source=col_at(d)).wait_recv()

    depth = 6 * bs
    everything = jnp.concatenate(
        [mine[s].reshape(depth, bs) for s in range(Y)], axis=1
    )

    for i in range(Y):
        part = lax.dot_general(
            mine[i].reshape(depth, bs),
            everything,
            (((0,), (0,)), ((), ())),
            preferred_element_type=F32,
        )
        for k in range(2):
            rows_k = slice(k * bs // 2, (k + 1) * bs // 2)
            for c in range(2):
                ssum[k, c, i] = part[rows_k, c * 2 * bs : (c + 1) * 2 * bs].astype(BF16)

    def sem(k, n):
        return s_sem.at[0, k, n], s_sem.at[1, k, n]

    chunks = range(2)
    copies = [
        send(ssum.at[k, 1 - core], half_recv.at[k], *sem(k, 0), (partner, y))
        for k in chunks
    ]
    after = []
    for k in chunks:
        copies[k].wait_recv()
        for i in range(Y):
            both = ssum[k, core, i].astype(F32) + half_recv[k, i].astype(F32)
            tsum[k, i] = both.astype(BF16)
        after.append(
            [
                send(tsum.at[k, col_at(d)], y_recv.at[k, Y - d], *sem(k, d), (r, col_at(d)))
                for d in range(1, Y)
            ]
        )
    copies, after = after, []
    for k in chunks:
        total = tsum[k, y].astype(F32)
        for copy in copies[k]:
            copy.wait_recv()
        for d in range(1, Y):
            total += y_recv[k, d].astype(F32)
        for i in range(X):
            usum[k, i] = total[i * piece : (i + 1) * piece].astype(BF16)
        after.append(
            [
                send(
                    usum.at[k, lax.rem(x + d, X)],
                    x_recv.at[k, X - d],
                    *sem(k, 3 + d),
                    (x_at(d, core), y),
                )
                for d in range(1, X)
            ]
        )
    copies, after = after, []
    for k in chunks:
        total = usum[k, x].astype(F32)
        for copy in copies[k]:
            copy.wait_recv()
        for d in range(1, X):
            total += x_recv[k, d].astype(F32)
        zsum[k] = total.astype(BF16)
        after.append(
            [
                send(zsum.at[k], z_recv.at[k, z], *sem(k, 6 + d), (z_at(d), y))
                for d in range(1, z_count)
            ]
        )
        z_recv[k, z] = total.astype(BF16)
    copies, after = after, []
    others = [(d, e) for d in range(X) for e in range(2) if d or e]
    for k in chunks:
        for copy in copies[k]:
            copy.wait_recv()
        total = z_recv[k, 0].astype(F32)
        for d in range(1, z_count):
            total += z_recv[k, d].astype(F32)
        final[k] = (total / norb).astype(BF16)
        after.append(
            [
                send(
                    final.at[k],
                    every.at[k, X - d if d else 0, e],
                    *sem(k, 14 + 2 * d + e),
                    (x_at(d, lax.rem(core + e, 2)), y),
                )
                for d, e in others
            ]
        )

    def place(k, xx, c, value):
        rows_k = pl.ds(pl.multiple_of(k * bs // 2 + xx * piece, piece), piece)
        columns_c = pl.ds(pl.multiple_of(c * 2 * bs, 2 * bs), 2 * bs)
        inter[rows_k, columns_c] = value.astype(F32)

    for k in chunks:
        place(k, x, core, final[k])
    for k in chunks:
        for copy in after[k]:
            copy.wait_recv()
        for d, e in others:
            back = X - d if d else 0
            place(k, lax.rem(x + back, X), lax.rem(core + e, 2), every[k, back, e])
    close()
    close_scatter()


def on_device(hamiltonian, block_column, vectors):
    bs = hamiltonian.shape[1]
    rows = lax.axis_size("row")
    z_count = rows // (2 * X)
    ham = hamiltonian.reshape(24, 12, bs, bs)
    vec = vectors.reshape(24, bs, bs)
    dma = pltpu.SemaphoreType.DMA
    any_spec = pl.BlockSpec(memory_space=pl.ANY)
    filtered, inter = pl.pallas_call(
        functools.partial(kernel, rows, float(rows * 24 * bs)),
        out_shape=(
            jax.ShapeDtypeStruct((24, bs, bs), BF16),
            jax.ShapeDtypeStruct((bs, Y * bs), F32),
        ),
        in_specs=[pl.BlockSpec(memory_space=pltpu.SMEM), any_spec, any_spec, any_spec],
        out_specs=(any_spec, pl.BlockSpec(memory_space=pltpu.VMEM)),
        scratch_shapes=[
            pltpu.VMEM((24, 12, bs, bs), BF16),
            pltpu.VMEM((STEPS + 1, 24, bs, bs), BF16),
            pltpu.VMEM((24, bs, bs), F32),
            pltpu.VMEM((4, 6, 2, bs, bs), BF16),
            pltpu.VMEM((STEPS, 4, 6, bs, bs), BF16),
            pltpu.VMEM((STEPS, 4, 6, bs, bs), BF16),
            pltpu.SMEM((4, 288), jnp.int32),
            pltpu.VMEM((Y, 6, bs, bs), BF16),
            pltpu.VMEM((2, Y, bs // 2, 2 * bs), BF16),
            pltpu.VMEM((2, Y, bs // 2, 2 * bs), BF16),
            pltpu.VMEM((2, Y, bs // 2, 2 * bs), BF16),
            pltpu.VMEM((2, X, bs // (2 * X), 2 * bs), BF16),
            pltpu.VMEM((2, X, bs // (2 * X), 2 * bs), BF16),
            pltpu.VMEM((2, bs // (2 * X), 2 * bs), BF16),
            pltpu.VMEM((2, z_count, bs // (2 * X), 2 * bs), BF16),
            pltpu.VMEM((2, bs // (2 * X), 2 * bs), BF16),
            pltpu.VMEM((2, X, 2, bs // (2 * X), 2 * bs), BF16),
            pltpu.VMEM((2, 2, Y, bs // 2, 2 * bs), BF16),
            dma((5,)),
            dma((2, 4)),
            dma((2, 7)),
            dma((2, 3, 4)),
            dma((2, STEPS, PARTS, 4)),
            dma((2, PARTS, 4)),
            dma((2, 2, 22)),
            dma((PARTS, 4)),
        ],
        compiler_params=pltpu.CompilerParams(
            collective_id=0, has_side_effects=True, vmem_limit_bytes=64 * 2**20 - 2**17
        ),
        name="chebyshev",
    )(block_column, block_column, ham, vec)
    return filtered.reshape(24 * bs, bs), inter


def solution(mesh):
    return jax.shard_map(
        on_device,
        mesh=mesh,
        in_specs=(P("row", None, None), P("row"), P("row", "col")),
        out_specs=(P("row", "col"), P("col", None)),
        check_vma=False,
    )
```

time: 387 us -> 84.5 us (0.22)
  waiting for transfers between devices: 263 us -> 0 us
  Pallas kernels: 0 us -> 79.9 us
  local copies, waits for them, and re-layouts: 37.2 us -> 3.73 us
  matrix products: 30.9 us -> 0 us
  starting transfers between devices: 30.8 us -> 0 us
  between operations: 14.1 us -> 0.64 us
  other arithmetic: 10.5 us -> 0 us
    psum x1 -> x0, waiting for transfers between devices: 178 us -> none  [on_device(): summed = lax.psum(partial_value, 'row')]
    pallas_call x0 -> x1, Pallas kernels: none -> 79.9 us  [on_device(): pl.pallas_call(functools.partial(kernel, rows, float(rows * 24 * bs)), ou...]
    all_gather x1 -> x0, waiting for transfers between devices: 52 us -> none  [on_device(): lax.all_gather(filtered, 'col', axis=1, tiled=True)]
    gather x6 -> x0, local copies, waits for them, and re-layouts: 36.9 us -> none  [the longest x3 26.4 us: operate(): gathered = jnp.concatenate([blocks[local_index], remote], axis=1)]
    ppermute x12 -> x0, waiting for transfers between devices: 33.7 us -> none  [from_behind(): return lax.ppermute(block, axis, route)]
    dot_general x4 -> x0, matrix products: 30.9 us -> none  [the longest x3 27.4 us: operate(): jnp.einsum('rqij,rqjk->rik', matrix_rows, gathered, preferred_element_typ...]
    ppermute x12 -> x0, starting transfers between devices: 30.7 us -> none  [from_behind(): return lax.ppermute(block, axis, route)]
    concatenate x3 -> x0, other arithmetic: 8.01 us -> none  [fetch_remote(): jnp.concatenate([from_behind(blocks, 'row', -offset) for offset in offset...]
  transfers between devices with their start and end apart: 14 -> 0, of which waited for: 11 -> 0; matrix products, arithmetic and copies ran while one was open for 7% -> 0% of each run, Pallas kernels for 0% -> 0%
where the time goes in v2:
time: 84.5 us; the launch traced here: 84.3 us
  Pallas kernels  79.9 us (95%)
  local copies, waits for them, and re-layouts  3.73 us (4%)
    pallas_call x1, Pallas kernels, on_device(): pl.pallas_call(functools.partial(kernel, rows, float(rows * 24 * bs)), ou...  79.9 us
    unnamed x2, local copies, waits for them, and re-layouts  3.73 us

profile of v2, /device:TPU:1, one launch (start us, length us, event | category | flops | bytes accessed | tf_op | source)
XLA Modules:
  0.0 84.3 jit_solution(1544109969462359932)
XLA Ops:
  0.6 79.9 %chebyshev.1 = (bf16[24,128,128]{2,1,0:T(8,128)(2,1)}, f32[128,512]{1,0:T(8,128)}) custom-call(s32[288]{0:T(512)} %bc_h.1, s32[288]{0:T(512)} %bc_h.1, bf16[24,12,128,128]{3,2,1,0:T(8,128)(2,1)} %bitcast.3, bf16[24,128,128]{2,1,0:T(8,128)(2,1)} %bitcast.4), custom_call_target="tpu_custom_call" | custom-call | tf_op jit(solution)/shard_map/chebyshev/pallas_call | solution.py:481
  80.6 2.1 %copy.7 = bf16[3072,128]{1,0:T(8,128)(2,1)} copy(bf16[3072,128]{1,0:T(8,128)(2,1)} %bitcast.5) | data formatting | bytes 1572864
  82.6 1.7 %copy.8 = f32[128,512]{1,0:T(8,128)} copy(f32[128,512]{1,0:T(8,128)} %get-tuple-element.9) | data formatting | bytes 524288

commit v3 on v2

--- a/solution.py
+++ b/solution.py
@@ -33,15 +33,15 @@
     vec,
     acc,
     hrem,
+    vsend,
+    vrecv,
     psend,
     precv,
     ridx,
     mine,
     half_recv,
     tsum,
-    y_recv,
-    usum,
-    x_recv,
+    yx_recv,
     zsum,
     z_recv,
     final,
@@ -51,6 +51,7 @@
     idx_sem,
     h_sem,
     fwd_sem,
+    v_sem,
     p_sem,
     a_sem,
     s_sem,
@@ -124,6 +125,7 @@
     peers += [(r, col_at(d)) for d in range(1, Y)]
     peers += [(x_at(d, c), y) for d in range(1, X) for c in range(2)]
     peers += [(z_at(d), y) for d in range(1, z_count)]
+    peers += [(x_at(d, core), col_at(e)) for d in range(1, X) for e in range(1, Y)]
     barrier = pltpu.get_barrier_semaphore()
     for peer in peers:
         pl.semaphore_signal(barrier, inc=1, device_id=peer, device_id_type=MESH)
@@ -136,13 +138,18 @@
     out_group = (1, 3, g_x_out)
     in_group = (1, 3, g_x_in)
 
-    def coupled_hbm(g, first, count):
-        return h_hbm.at[pl.ds(6 * g + first, count), pl.ds(10, 2)]
+    idx_copies = [
+        send(bc_h, ridx.at[g], idx_sem.at[0, g], idx_sem.at[1, g], (row_at(OFFSETS[g]), y))
+        for g in range(4)
+    ]
+
+    def rows_of(owner):
+        return pl.ds(pl.multiple_of(owner * bs // Y, bs // Y), bs // Y)
 
     quarter_copies = [
         send(
-            coupled_hbm(g, y, 1),
-            hrem.at[g, pl.ds(y, 1)],
+            h_hbm.at[pl.ds(6 * g, 6), pl.ds(10, 2), rows_of(y)],
+            hrem.at[g, :, :, rows_of(y)],
             h_sem.at[0, j],
             h_sem.at[1, j],
             (to_row[j], y),
@@ -156,21 +163,6 @@
         h_sem.at[1, 3],
         (partner, y),
     )
-    idx_copies = [
-        send(bc_h, ridx.at[g], idx_sem.at[0, g], idx_sem.at[1, g], (row_at(OFFSETS[g]), y))
-        for g in range(4)
-    ]
-    lower_copies = [
-        send(
-            coupled_hbm(g, Y, 2),
-            hrem.at[g, pl.ds(Y, 2)],
-            h_sem.at[0, 4 + j],
-            h_sem.at[1, 4 + j],
-            (to_row[j], y),
-        )
-        for j, g in enumerate(out_group)
-    ]
-
     for g in range(1, 4):
         load_rows(g)
 
@@ -196,7 +188,7 @@
                 ],
                 axis=0,
             )
-            psend[step, g, i] = jnp.dot(lhs, rhs, preferred_element_type=F32).astype(BF16)
+            psend[step - 1, g, i] = jnp.dot(lhs, rhs, preferred_element_type=F32).astype(BF16)
             return carry
 
         lax.fori_loop(0, 6, body, 0, unroll=6)
@@ -207,10 +199,10 @@
     def product_copy(step, g, h, peer):
         part = pl.ds(PER_PART * h, PER_PART)
         return (
-            psend.at[step, g, part],
-            precv.at[step, g, part],
-            p_sem.at[0, step, h, g],
-            p_sem.at[1, step, h, g],
+            psend.at[step - 1, g, part],
+            precv.at[step - 1, g, part],
+            p_sem.at[0, step - 1, h, g],
+            p_sem.at[1, step - 1, h, g],
             peer,
         )
 
@@ -218,13 +210,41 @@
         send(*product_copy(step, in_groups[j], h, (back_to[j], y)))
 
     loaded("vec")
+
+    def vector_copy(g, h, peer):
+        part = pl.ds(2 * PER_PART * h, 2 * PER_PART)
+        return (
+            vsend.at[g, part],
+            vrecv.at[g, part],
+            v_sem.at[0, h, g],
+            v_sem.at[1, h, g],
+            peer,
+        )
+
+    for copy in idx_copies:
+        copy.wait_recv()
+    for j in (0, 1, 3, 2):
+        g = in_groups[j]
+
+        def pick(i, carry, g=g):
+            for q in range(2):
+                entry = inside(ridx[g, (6 * g + i) * 12 + 10 + q])
+                vsend[g, 2 * i + q] = vec[0, entry]
+            return carry
+
+        lax.fori_loop(0, 6, pick, 0, unroll=2)
+        for h in range(PARTS):
+            send(*vector_copy(g, h, (back_to[j], y)))
+
     loaded(0)
-    local_rows(0, 0, 6, 6)
+    local_rows(0, 0, 6, 2)
+    loaded(1)
+    local_rows(0, 6, 6, 2)
 
     fwd = []
     for j in range(3):
         quarter_copies[j].wait_recv()
-        part = hrem.at[in_group[j], pl.ds(y, 1)]
+        part = hrem.at[in_group[j], :, :, rows_of(y)]
         fwd.append(
             [
                 send(
@@ -237,16 +257,16 @@
                 for side, d in enumerate((1, -1))
             ]
         )
-
-    loaded(1)
-    local_rows(0, 6, 6, 6)
-
+    loaded(2)
+    local_rows(0, 12, 6, 2)
+    loaded(3)
+    local_rows(0, 18, 6, 2)
     second = []
     for j in range(3):
         pair = []
         for side, d in enumerate((1, -1)):
             fwd[j][side].wait_recv()
-            part = hrem.at[in_group[j], pl.ds(col_at(-d), 1), pl.ds(side, 1)]
+            part = hrem.at[in_group[j], :, pl.ds(side, 1), rows_of(col_at(-d))]
             pair.append(
                 send(
                     part,
@@ -257,20 +277,22 @@
                 )
             )
         second.append(pair)
-        if j < 2:
-            loaded(2 + j)
-            local_rows(0, 12 + 6 * j, 6, 6)
-
-    for copy in idx_copies:
-        copy.wait_recv()
-
 
     def finish(step, g, h):
-        remote(*product_copy(step, g, h, (partner, y))).wait_recv()
+        args = vector_copy if step == 0 else functools.partial(product_copy, step)
+        remote(*args(g, h, (partner, y))).wait_recv()
 
         def body(i, carry):
             b = 6 * g + PER_PART * h + i
-            product = acc[b] + precv[step, g, PER_PART * h + i].astype(F32)
+            n = PER_PART * h + i
+            if step == 0:
+                product = acc[b] + jnp.dot(
+                    jnp.concatenate([ham[b, 10], ham[b, 11]], axis=1),
+                    jnp.concatenate([vrecv[g, 2 * n], vrecv[g, 2 * n + 1]], axis=0),
+                    preferred_element_type=F32,
+                )
+            else:
+                product = acc[b] + precv[step - 1, g, n].astype(F32)
             shifted = product - CENTER * vec[step, b].astype(F32)
             if step == 0:
                 vec[1, b] = (shifted / HALF).astype(BF16)
@@ -322,24 +344,21 @@
             if step == STEPS - 1:
                 scatter(g, h)
 
-        if step == 0:
-            for j in range(3):
-                for copy in (*second[j], lower_copies[j]):
-                    copy.wait_recv()
-                products(0, in_groups[j])
-                for h in parts:
-                    send_products(0, j, h)
-            chip_copy.wait_recv()
-            products(0, g_chip_in)
-            for h in parts:
-                send_products(0, 3, h)
-        else:
+        if step > 0:
+            if step == 1:
+                for j in (0, 1):
+                    for copy in second[j]:
+                        copy.wait_recv()
+                chip_copy.wait_recv()
             for j in (0, 1):
                 products(step, in_groups[j])
                 send_products(step, j, 0)
             products(step, g_chip_in)
             for h in parts:
                 send_products(step, 3, h)
+            if step == 1:
+                for copy in second[2]:
+                    copy.wait_recv()
             products(step, in_groups[2])
             send_products(step, 2, 0)
             for h in parts[1:]:
@@ -380,6 +399,11 @@
     def sem(k, n):
         return s_sem.at[0, k, n], s_sem.at[1, k, n]
 
+    def far_first(size):
+        return sorted(range(1, size), key=lambda d: -min(d, size - d))
+
+    offsets = [(d, e) for d in range(Y) for e in range(X) if d or e]
+    offsets.sort(key=lambda o: -min(o[0], Y - o[0]) - min(o[1], X - o[1]))
     chunks = range(2)
     copies = [
         send(ssum.at[k, 1 - core], half_recv.at[k], *sem(k, 0), (partner, y))
@@ -390,45 +414,31 @@
         copies[k].wait_recv()
         for i in range(Y):
             both = ssum[k, core, i].astype(F32) + half_recv[k, i].astype(F32)
-            tsum[k, i] = both.astype(BF16)
-        after.append(
-            [
-                send(tsum.at[k, col_at(d)], y_recv.at[k, Y - d], *sem(k, d), (r, col_at(d)))
-                for d in range(1, Y)
-            ]
-        )
-    copies, after = after, []
-    for k in chunks:
-        total = tsum[k, y].astype(F32)
-        for copy in copies[k]:
-            copy.wait_recv()
-        for d in range(1, Y):
-            total += y_recv[k, d].astype(F32)
-        for i in range(X):
-            usum[k, i] = total[i * piece : (i + 1) * piece].astype(BF16)
+            for j in range(X):
+                tsum[k, i, j] = both[j * piece : (j + 1) * piece].astype(BF16)
         after.append(
             [
                 send(
-                    usum.at[k, lax.rem(x + d, X)],
-                    x_recv.at[k, X - d],
-                    *sem(k, 3 + d),
-                    (x_at(d, core), y),
+                    tsum.at[k, col_at(d), lax.rem(x + e, X)],
+                    yx_recv.at[k, (-d % Y) * X + -e % X],
+                    *sem(k, d * X + e),
+                    (x_at(e, core), col_at(d)),
                 )
-                for d in range(1, X)
+                for d, e in offsets
             ]
         )
     copies, after = after, []
     for k in chunks:
-        total = usum[k, x].astype(F32)
+        total = tsum[k, y, x].astype(F32)
         for copy in copies[k]:
             copy.wait_recv()
-        for d in range(1, X):
-            total += x_recv[k, d].astype(F32)
+        for n in range(1, Y * X):
+            total += yx_recv[k, n].astype(F32)
         zsum[k] = total.astype(BF16)
         after.append(
             [
-                send(zsum.at[k], z_recv.at[k, z], *sem(k, 6 + d), (z_at(d), y))
-                for d in range(1, z_count)
+                send(zsum.at[k], z_recv.at[k, z], *sem(k, Y * X + d), (z_at(d), y))
+                for d in far_first(z_count)
             ]
         )
         z_recv[k, z] = total.astype(BF16)
@@ -446,7 +456,7 @@
                 send(
                     final.at[k],
                     every.at[k, X - d if d else 0, e],
-                    *sem(k, 14 + 2 * d + e),
+                    *sem(k, Y * X + z_count + 2 * d + e),
                     (x_at(d, lax.rem(core + e, 2)), y),
                 )
                 for d, e in others
@@ -491,15 +501,15 @@
             pltpu.VMEM((STEPS + 1, 24, bs, bs), BF16),
             pltpu.VMEM((24, bs, bs), F32),
             pltpu.VMEM((4, 6, 2, bs, bs), BF16),
-            pltpu.VMEM((STEPS, 4, 6, bs, bs), BF16),
-            pltpu.VMEM((STEPS, 4, 6, bs, bs), BF16),
+            pltpu.VMEM((4, 12, bs, bs), BF16),
+            pltpu.VMEM((4, 12, bs, bs), BF16),
+            pltpu.VMEM((STEPS - 1, 4, 6, bs, bs), BF16),
+            pltpu.VMEM((STEPS - 1, 4, 6, bs, bs), BF16),
             pltpu.SMEM((4, 288), jnp.int32),
             pltpu.VMEM((Y, 6, bs, bs), BF16),
             pltpu.VMEM((2, Y, bs // 2, 2 * bs), BF16),
-            pltpu.VMEM((2, Y, bs // 2, 2 * bs), BF16),
-            pltpu.VMEM((2, Y, bs // 2, 2 * bs), BF16),
-            pltpu.VMEM((2, X, bs // (2 * X), 2 * bs), BF16),
-            pltpu.VMEM((2, X, bs // (2 * X), 2 * bs), BF16),
+            pltpu.VMEM((2, Y, X, bs // (2 * X), 2 * bs), BF16),
+            pltpu.VMEM((2, Y * X, bs // (2 * X), 2 * bs), BF16),
             pltpu.VMEM((2, bs // (2 * X), 2 * bs), BF16),
             pltpu.VMEM((2, z_count, bs // (2 * X), 2 * bs), BF16),
             pltpu.VMEM((2, bs // (2 * X), 2 * bs), BF16),
@@ -507,11 +517,12 @@
             pltpu.VMEM((2, 2, Y, bs // 2, 2 * bs), BF16),
             dma((5,)),
             dma((2, 4)),
-            dma((2, 7)),
+            dma((2, 4)),
             dma((2, 3, 4)),
-            dma((2, STEPS, PARTS, 4)),
             dma((2, PARTS, 4)),
-            dma((2, 2, 22)),
+            dma((2, STEPS - 1, PARTS, 4)),
+            dma((2, PARTS, 4)),
+            dma((2, 2, Y * X + z_count + 2 * X)),
             dma((PARTS, 4)),
         ],
         compiler_params=pltpu.CompilerParams(

time: 84.5 us -> 81.9 us (0.969)
  Pallas kernels: 79.9 us -> 77.4 us
    pallas_call x1, Pallas kernels: 79.9 us -> 77.4 us  [on_device(): pl.pallas_call(functools.partial(kernel, rows, float(rows * 24 * bs)), ou...]
where the time goes in v3:
time: 81.9 us; the launch traced here: 81.8 us
  Pallas kernels  77.4 us (95%)
  local copies, waits for them, and re-layouts  3.73 us (5%)
    pallas_call x1, Pallas kernels, on_device(): pl.pallas_call(functools.partial(kernel, rows, float(rows * 24 * bs)), ou...  77.4 us
    unnamed x2, local copies, waits for them, and re-layouts  3.73 us

profile of v3, /device:TPU:1, one launch (start us, length us, event | category | flops | bytes accessed | tf_op | source)
XLA Modules:
  0.0 81.8 jit_solution(5538053912961632118)
XLA Ops:
  0.6 77.4 %chebyshev.1 = (bf16[24,128,128]{2,1,0:T(8,128)(2,1)}, f32[128,512]{1,0:T(8,128)}) custom-call(s32[288]{0:T(512)} %bc_h.1, s32[288]{0:T(512)} %bc_h.1, bf16[24,12,128,128]{3,2,1,0:T(8,128)(2,1)} %bitcast.3, bf16[24,128,128]{2,1,0:T(8,128)(2,1)} %bitcast.4), custom_call_target="tpu_custom_call" | custom-call | tf_op jit(solution)/shard_map/chebyshev/pallas_call | solution.py:491
  78.0 2.1 %copy.7 = bf16[3072,128]{1,0:T(8,128)(2,1)} copy(bf16[3072,128]{1,0:T(8,128)(2,1)} %bitcast.5) | data formatting | bytes 1572864
  80.1 1.7 %copy.8 = f32[128,512]{1,0:T(8,128)} copy(f32[128,512]{1,0:T(8,128)} %get-tuple-element.9) | data formatting | bytes 524288

commit v4 on v3

--- a/solution.py
+++ b/solution.py
@@ -16,8 +16,9 @@
 HALF = 0.8
 X = 4
 Y = 4
-PARTS = 3
-PER_PART = 6 // PARTS
+PARTS = (1, 2, 3)
+MOST = max(PARTS)
+CHUNKS = 1
 
 
 def kernel(
@@ -64,7 +65,7 @@
     x = lax.rem(r // 2, X)
     z = r // (2 * X)
     bs = ham.shape[-1]
-    piece = bs // (2 * X)
+    piece = bs // (CHUNKS * X)
     base = r * 24
 
     def inside(entry):
@@ -197,7 +198,7 @@
     back_to = (row_at(-2), row_at(2), lax.rem(r + 2 * core - 1 + rows, rows), partner)
 
     def product_copy(step, g, h, peer):
-        part = pl.ds(PER_PART * h, PER_PART)
+        part = part_of(step, h)
         return (
             psend.at[step - 1, g, part],
             precv.at[step - 1, g, part],
@@ -211,8 +212,12 @@
 
     loaded("vec")
 
+    def part_of(step, h, each=1, first=0):
+        count = 6 // PARTS[step]
+        return pl.ds(first + each * count * h, each * count)
+
     def vector_copy(g, h, peer):
-        part = pl.ds(2 * PER_PART * h, 2 * PER_PART)
+        part = part_of(0, h, 2)
         return (
             vsend.at[g, part],
             vrecv.at[g, part],
@@ -233,7 +238,7 @@
             return carry
 
         lax.fori_loop(0, 6, pick, 0, unroll=2)
-        for h in range(PARTS):
+        for h in range(PARTS[0]):
             send(*vector_copy(g, h, (back_to[j], y)))
 
     loaded(0)
@@ -283,8 +288,8 @@
         remote(*args(g, h, (partner, y))).wait_recv()
 
         def body(i, carry):
-            b = 6 * g + PER_PART * h + i
-            n = PER_PART * h + i
+            n = 6 // PARTS[step] * h + i
+            b = 6 * g + n
             if step == 0:
                 product = acc[b] + jnp.dot(
                     jnp.concatenate([ham[b, 10], ham[b, 11]], axis=1),
@@ -302,20 +307,16 @@
                 ).astype(BF16)
             return carry
 
-        lax.fori_loop(0, PER_PART, body, 0, unroll=PER_PART)
+        lax.fori_loop(0, 6 // PARTS[step], body, 0, unroll=2 if PARTS[step] == 3 else 3)
 
     def to_mine(g, h, source=y, local=False):
-        group = vec.at[STEPS, pl.ds(6 * g + PER_PART * h, PER_PART)]
-        place = mine.at[source, pl.ds(PER_PART * h, PER_PART)]
+        group = vec.at[STEPS, part_of(-1, h, first=6 * g)]
+        place = mine.at[source, part_of(-1, h)]
         if local:
             return pltpu.make_async_copy(group, place, a_sem.at[1, h, y])
         return remote(group, place, a_sem.at[0, h, g], a_sem.at[1, h, source], (r, g))
 
-    def to_hbm(g, h):
-        rows_g = pl.ds(6 * g + PER_PART * h, PER_PART)
-        return pltpu.make_async_copy(
-            vec.at[STEPS, rows_g], f_hbm.at[rows_g], out_sem.at[h, g]
-        )
+    to_hbm = pltpu.make_async_copy(vec.at[STEPS], f_hbm, out_sem)
 
     def scatter(g, h):
         @pl.when(g != y)
@@ -326,18 +327,15 @@
         def _():
             to_mine(g, h, local=True).start()
 
-        to_hbm(g, h).start()
-
     def close_scatter():
-        for h in range(PARTS):
+        for h in range(PARTS[-1]):
             for d in range(1, Y):
                 to_mine(col_at(d), h).wait_send()
-            for g in range(4):
-                to_hbm(g, h).wait()
+        to_hbm.wait()
 
     own_groups = (1, 3, g_x_out)
-    parts = range(PARTS)
     for step in range(STEPS):
+        parts = range(PARTS[step])
 
         def complete(g, h, step=step):
             finish(step, g, h)
@@ -374,7 +372,8 @@
             for g in own_groups:
                 complete(g, h)
 
-    for h in parts:
+    to_hbm.start()
+    for h in range(PARTS[-1]):
         to_mine(y, h, local=True).wait()
         for d in range(1, Y):
             to_mine(col_at(d), h, source=col_at(d)).wait_recv()
@@ -391,8 +390,8 @@
             (((0,), (0,)), ((), ())),
             preferred_element_type=F32,
         )
-        for k in range(2):
-            rows_k = slice(k * bs // 2, (k + 1) * bs // 2)
+        for k in range(CHUNKS):
+            rows_k = slice(k * bs // CHUNKS, (k + 1) * bs // CHUNKS)
             for c in range(2):
                 ssum[k, c, i] = part[rows_k, c * 2 * bs : (c + 1) * 2 * bs].astype(BF16)
 
@@ -404,7 +403,7 @@
 
     offsets = [(d, e) for d in range(Y) for e in range(X) if d or e]
     offsets.sort(key=lambda o: -min(o[0], Y - o[0]) - min(o[1], X - o[1]))
-    chunks = range(2)
+    chunks = range(CHUNKS)
     copies = [
         send(ssum.at[k, 1 - core], half_recv.at[k], *sem(k, 0), (partner, y))
         for k in chunks
@@ -464,7 +463,7 @@
         )
 
     def place(k, xx, c, value):
-        rows_k = pl.ds(pl.multiple_of(k * bs // 2 + xx * piece, piece), piece)
+        rows_k = pl.ds(pl.multiple_of(k * bs // CHUNKS + xx * piece, piece), piece)
         columns_c = pl.ds(pl.multiple_of(c * 2 * bs, 2 * bs), 2 * bs)
         inter[rows_k, columns_c] = value.astype(F32)
 
@@ -480,10 +479,25 @@
     close_scatter()
 
 
+def publish(f_from, inter_from, f_to, inter_to, f_held, inter_held, copy_sem):
+    pairs = [(f_from, f_held), (inter_from, inter_held), (f_held, f_to), (inter_held, inter_to)]
+    copies = [
+        pltpu.make_async_copy(src, dst, copy_sem.at[n]) for n, (src, dst) in enumerate(pairs)
+    ]
+    for n in (0, 1):
+        copies[n].start()
+    for n in (0, 1):
+        copies[n].wait()
+        copies[2 + n].start()
+    for n in (2, 3):
+        copies[n].wait()
+
+
 def on_device(hamiltonian, block_column, vectors):
     bs = hamiltonian.shape[1]
     rows = lax.axis_size("row")
     z_count = rows // (2 * X)
+    piece = bs // (CHUNKS * X)
     ham = hamiltonian.reshape(24, 12, bs, bs)
     vec = vectors.reshape(24, bs, bs)
     dma = pltpu.SemaphoreType.DMA
@@ -507,29 +521,45 @@
             pltpu.VMEM((STEPS - 1, 4, 6, bs, bs), BF16),
             pltpu.SMEM((4, 288), jnp.int32),
             pltpu.VMEM((Y, 6, bs, bs), BF16),
-            pltpu.VMEM((2, Y, bs // 2, 2 * bs), BF16),
-            pltpu.VMEM((2, Y, X, bs // (2 * X), 2 * bs), BF16),
-            pltpu.VMEM((2, Y * X, bs // (2 * X), 2 * bs), BF16),
-            pltpu.VMEM((2, bs // (2 * X), 2 * bs), BF16),
-            pltpu.VMEM((2, z_count, bs // (2 * X), 2 * bs), BF16),
-            pltpu.VMEM((2, bs // (2 * X), 2 * bs), BF16),
-            pltpu.VMEM((2, X, 2, bs // (2 * X), 2 * bs), BF16),
-            pltpu.VMEM((2, 2, Y, bs // 2, 2 * bs), BF16),
+            pltpu.VMEM((CHUNKS, Y, bs // CHUNKS, 2 * bs), BF16),
+            pltpu.VMEM((CHUNKS, Y, X, piece, 2 * bs), BF16),
+            pltpu.VMEM((CHUNKS, Y * X, piece, 2 * bs), BF16),
+            pltpu.VMEM((CHUNKS, piece, 2 * bs), BF16),
+            pltpu.VMEM((CHUNKS, z_count, piece, 2 * bs), BF16),
+            pltpu.VMEM((CHUNKS, piece, 2 * bs), BF16),
+            pltpu.VMEM((CHUNKS, X, 2, piece, 2 * bs), BF16),
+            pltpu.VMEM((CHUNKS, 2, Y, bs // CHUNKS, 2 * bs), BF16),
             dma((5,)),
             dma((2, 4)),
             dma((2, 4)),
             dma((2, 3, 4)),
-            dma((2, PARTS, 4)),
-            dma((2, STEPS - 1, PARTS, 4)),
-            dma((2, PARTS, 4)),
-            dma((2, 2, Y * X + z_count + 2 * X)),
-            dma((PARTS, 4)),
+            dma((2, MOST, 4)),
+            dma((2, STEPS - 1, MOST, 4)),
+            dma((2, MOST, 4)),
+            dma((2, CHUNKS, Y * X + z_count + 2 * X)),
+            dma,
         ],
         compiler_params=pltpu.CompilerParams(
             collective_id=0, has_side_effects=True, vmem_limit_bytes=64 * 2**20 - 2**17
         ),
         name="chebyshev",
     )(block_column, block_column, ham, vec)
+    filtered, inter = pl.pallas_call(
+        publish,
+        out_shape=(
+            jax.ShapeDtypeStruct((24, bs, bs), BF16),
+            jax.ShapeDtypeStruct((bs, Y * bs), F32),
+        ),
+        in_specs=[any_spec] * 2,
+        out_specs=(any_spec, any_spec),
+        scratch_shapes=[
+            pltpu.VMEM((24, bs, bs), BF16),
+            pltpu.VMEM((bs, Y * bs), F32),
+            dma((4,)),
+        ],
+        compiler_params=pltpu.CompilerParams(vmem_limit_bytes=64 * 2**20 - 2**17),
+        name="publish",
+    )(filtered, inter)
     return filtered.reshape(24 * bs, bs), inter
 
 

time: 81.9 us -> 79.7 us (0.973)
  local copies, waits for them, and re-layouts: 3.73 us -> 0 us
  Pallas kernels: 77.4 us -> 79 us
    unnamed x2 -> x0, local copies, waits for them, and re-layouts: 3.73 us -> none
    pallas_call x0 -> x1, Pallas kernels: none -> 2.13 us  [on_device(): pl.pallas_call(publish, out_shape=(jax.ShapeDtypeStruct((24, bs, bs), BF1...]
where the time goes in v4:
time: 79.7 us; the launch traced here: 79.6 us
  Pallas kernels  79 us (99%)
    pallas_call x1, Pallas kernels, on_device(): pl.pallas_call(functools.partial(kernel, rows, float(rows * 24 * bs)), ou...  76.8 us
    pallas_call x1, Pallas kernels, on_device(): pl.pallas_call(publish, out_shape=(jax.ShapeDtypeStruct((24, bs, bs), BF1...  2.13 us

profile of v4, /device:TPU:1, one launch (start us, length us, event | category | flops | bytes accessed | tf_op | source)
XLA Modules:
  0.0 79.6 jit_solution(10515961929110642589)
XLA Ops:
  0.6 76.8 %chebyshev.1 = (bf16[24,128,128]{2,1,0:T(8,128)(2,1)}, f32[128,512]{1,0:T(8,128)}) custom-call(s32[288]{0:T(512)} %bc_h.1, s32[288]{0:T(512)} %bc_h.1, bf16[24,12,128,128]{3,2,1,0:T(8,128)(2,1)} %bitcast.3, bf16[24,128,128]{2,1,0:T(8,128)(2,1)} %bitcast.4), custom_call_target="tpu_custom_call" | custom-call | tf_op jit(solution)/shard_map/chebyshev/pallas_call | solution.py:505
  77.5 2.1 %publish.1 = (bf16[24,128,128]{2,1,0:T(8,128)(2,1)}, f32[128,512]{1,0:T(8,128)}) custom-call(bf16[24,128,128]{2,1,0:T(8,128)(2,1)} %get-tuple-element.6.f_from, f32[128,512]{1,0:T(8,128)} %get-tuple-element.7.inter_from), custom_call_target="tpu_custom_call" | custom-call | tf_op jit(solution)/shard_map/publish/pallas_call | solution.py:547

commit v5 on v4

--- a/solution.py
+++ b/solution.py
@@ -16,7 +16,7 @@
 HALF = 0.8
 X = 4
 Y = 4
-PARTS = (1, 2, 3)
+PARTS = (1, 1, 3)
 MOST = max(PARTS)
 CHUNKS = 1
 
@@ -109,18 +109,16 @@
         sends.append(copy)
         return copy
 
+    def drain(count=None):
+        done = sends[:count]
+        del sends[:count]
+        for copy in done:
+            copy.wait_send()
+
     def close():
-        for copy in sends:
-            copy.wait_send()
+        drain()
         for name in tuple(loads):
             loaded(name)
-
-    load("vec", v_hbm, vec.at[0], load_sem.at[4])
-
-    def load_rows(g):
-        load(g, h_hbm.at[pl.ds(6 * g, 6)], ham.at[pl.ds(6 * g, 6)], load_sem.at[g])
-
-    load_rows(0)
 
     peers = [(row_at(o), y) for o in OFFSETS]
     peers += [(r, col_at(d)) for d in range(1, Y)]
@@ -130,6 +128,12 @@
     barrier = pltpu.get_barrier_semaphore()
     for peer in peers:
         pl.semaphore_signal(barrier, inc=1, device_id=peer, device_id_type=MESH)
+    load("vec", v_hbm, vec.at[0], load_sem.at[4])
+
+    def load_rows(g):
+        load(g, h_hbm.at[pl.ds(6 * g, 6)], ham.at[pl.ds(6 * g, 6)], load_sem.at[g])
+
+    load_rows(0)
     pl.semaphore_wait(barrier, len(peers))
 
     g_x_out, g_chip_out = 2 * (1 - core), 2 * core
@@ -331,11 +335,11 @@
         for h in range(PARTS[-1]):
             for d in range(1, Y):
                 to_mine(col_at(d), h).wait_send()
-        to_hbm.wait()
 
     own_groups = (1, 3, g_x_out)
     for step in range(STEPS):
         parts = range(PARTS[step])
+        before = len(sends) if step else 8
 
         def complete(g, h, step=step):
             finish(step, g, h)
@@ -368,11 +372,13 @@
         if step > 0:
             for g in own_groups:
                 local_rows(step, 6 * g, 6, 6)
+        drain(before)
         for h in parts:
             for g in own_groups:
                 complete(g, h)
 
     to_hbm.start()
+    drain()
     for h in range(PARTS[-1]):
         to_mine(y, h, local=True).wait()
         for d in range(1, Y):
@@ -426,6 +432,7 @@
                 for d, e in offsets
             ]
         )
+    close_scatter()
     copies, after = after, []
     for k in chunks:
         total = tsum[k, y, x].astype(F32)
@@ -441,6 +448,7 @@
             ]
         )
         z_recv[k, z] = total.astype(BF16)
+    drain(1 + len(offsets) * CHUNKS)
     copies, after = after, []
     others = [(d, e) for d in range(X) for e in range(2) if d or e]
     for k in chunks:
@@ -469,6 +477,8 @@
 
     for k in chunks:
         place(k, x, core, final[k])
+    drain((z_count - 1) * CHUNKS)
+    to_hbm.wait()
     for k in chunks:
         for copy in after[k]:
             copy.wait_recv()
@@ -476,21 +486,25 @@
             back = X - d if d else 0
             place(k, lax.rem(x + back, X), lax.rem(core + e, 2), every[k, back, e])
     close()
-    close_scatter()
 
 
 def publish(f_from, inter_from, f_to, inter_to, f_held, inter_held, copy_sem):
-    pairs = [(f_from, f_held), (inter_from, inter_held), (f_held, f_to), (inter_held, inter_to)]
-    copies = [
-        pltpu.make_async_copy(src, dst, copy_sem.at[n]) for n, (src, dst) in enumerate(pairs)
+    halves = [pl.ds(0, 12), pl.ds(12, 12)]
+    arrays = [(f_from.at[h], f_held.at[h], f_to.at[h]) for h in halves]
+    arrays.append((inter_from, inter_held, inter_to))
+    inward = [
+        pltpu.make_async_copy(a, b, copy_sem.at[0, n]) for n, (a, b, _) in enumerate(arrays)
     ]
-    for n in (0, 1):
-        copies[n].start()
-    for n in (0, 1):
-        copies[n].wait()
-        copies[2 + n].start()
-    for n in (2, 3):
-        copies[n].wait()
+    outward = [
+        pltpu.make_async_copy(b, c, copy_sem.at[1, n]) for n, (_, b, c) in enumerate(arrays)
+    ]
+    for copy in inward:
+        copy.start()
+    for first, then in zip(inward, outward):
+        first.wait()
+        then.start()
+    for copy in outward:
+        copy.wait()
 
 
 def on_device(hamiltonian, block_column, vectors):
@@ -555,7 +569,7 @@
         scratch_shapes=[
             pltpu.VMEM((24, bs, bs), BF16),
             pltpu.VMEM((bs, Y * bs), F32),
-            dma((4,)),
+            dma((2, 3)),
         ],
         compiler_params=pltpu.CompilerParams(vmem_limit_bytes=64 * 2**20 - 2**17),
         name="publish",

time: 79.7 us -> 78.1 us (0.980)
  Pallas kernels: 79 us -> 77.3 us
    pallas_call x1, Pallas kernels: 76.8 us -> 75.3 us  [on_device(): pl.pallas_call(functools.partial(kernel, rows, float(rows * 24 * bs)), ou...]
where the time goes in v5:
time: 78.1 us; the launch traced here: 77.9 us
  Pallas kernels  77.3 us (99%)
    pallas_call x1, Pallas kernels, on_device(): pl.pallas_call(functools.partial(kernel, rows, float(rows * 24 * bs)), ou...  75.3 us
    pallas_call x1, Pallas kernels, on_device(): pl.pallas_call(publish, out_shape=(jax.ShapeDtypeStruct((24, bs, bs), BF1...  2.01 us

profile of v5, /device:TPU:1, one launch (start us, length us, event | category | flops | bytes accessed | tf_op | source)
XLA Modules:
  0.0 77.9 jit_solution(7898789058171617577)
XLA Ops:
  0.6 75.3 %chebyshev.1 = (bf16[24,128,128]{2,1,0:T(8,128)(2,1)}, f32[128,512]{1,0:T(8,128)}) custom-call(s32[288]{0:T(512)} %bc_h.1, s32[288]{0:T(512)} %bc_h.1, bf16[24,12,128,128]{3,2,1,0:T(8,128)(2,1)} %bitcast.3, bf16[24,128,128]{2,1,0:T(8,128)(2,1)} %bitcast.4), custom_call_target="tpu_custom_call" | custom-call | tf_op jit(solution)/shard_map/chebyshev/pallas_call | solution.py:519
  75.9 2.0 %publish.1 = (bf16[24,128,128]{2,1,0:T(8,128)(2,1)}, f32[128,512]{1,0:T(8,128)}) custom-call(bf16[24,128,128]{2,1,0:T(8,128)(2,1)} %get-tuple-element.6.f_from, f32[128,512]{1,0:T(8,128)} %get-tuple-element.7.inter_from), custom_call_target="tpu_custom_call" | custom-call | tf_op jit(solution)/shard_map/publish/pallas_call | solution.py:561

commit v6 on v5

--- a/solution.py
+++ b/solution.py
@@ -171,6 +171,9 @@
     for g in range(1, 4):
         load_rows(g)
 
+    def scale(step):
+        return (2.0 if step else 1.0) / HALF
+
     def local_rows(current, first_row, count, unroll):
         def body(i, carry):
             b = first_row + i
@@ -178,7 +181,11 @@
             rhs = jnp.concatenate(
                 [vec[current, inside(bc_s[b * 12 + k])] for k in range(10)], axis=0
             )
-            acc[b] = jnp.dot(lhs, rhs, preferred_element_type=F32)
+            product = jnp.dot(lhs, rhs, preferred_element_type=F32)
+            shifted = scale(current) * (product - CENTER * vec[current, b].astype(F32))
+            if current > 0:
+                shifted = shifted - vec[current - 1, b].astype(F32)
+            acc[b] = shifted
             return carry
 
         lax.fori_loop(0, count, body, 0, unroll=unroll)
@@ -295,20 +302,14 @@
             n = 6 // PARTS[step] * h + i
             b = 6 * g + n
             if step == 0:
-                product = acc[b] + jnp.dot(
+                product = jnp.dot(
                     jnp.concatenate([ham[b, 10], ham[b, 11]], axis=1),
                     jnp.concatenate([vrecv[g, 2 * n], vrecv[g, 2 * n + 1]], axis=0),
                     preferred_element_type=F32,
                 )
             else:
-                product = acc[b] + precv[step - 1, g, n].astype(F32)
-            shifted = product - CENTER * vec[step, b].astype(F32)
-            if step == 0:
-                vec[1, b] = (shifted / HALF).astype(BF16)
-            else:
-                vec[step + 1, b] = (
-                    2.0 * shifted / HALF - vec[step - 1, b].astype(F32)
-                ).astype(BF16)
+                product = precv[step - 1, g, n].astype(F32)
+            vec[step + 1, b] = (acc[b] + scale(step) * product).astype(BF16)
             return carry
 
         lax.fori_loop(0, 6 // PARTS[step], body, 0, unroll=2 if PARTS[step] == 3 else 3)
@@ -385,21 +386,23 @@
             to_mine(col_at(d), h, source=col_at(d)).wait_recv()
 
     depth = 6 * bs
-    everything = jnp.concatenate(
-        [mine[s].reshape(depth, bs) for s in range(Y)], axis=1
-    )
-
-    for i in range(Y):
-        part = lax.dot_general(
-            mine[i].reshape(depth, bs),
-            everything,
-            (((0,), (0,)), ((), ())),
-            preferred_element_type=F32,
-        )
-        for k in range(CHUNKS):
-            rows_k = slice(k * bs // CHUNKS, (k + 1) * bs // CHUNKS)
-            for c in range(2):
-                ssum[k, c, i] = part[rows_k, c * 2 * bs : (c + 1) * 2 * bs].astype(BF16)
+
+    def sums(c):
+        columns = jnp.concatenate(
+            [mine[2 * c + s].reshape(depth, bs) for s in range(2)], axis=1
+        )
+        for i in range(Y):
+            part = lax.dot_general(
+                mine[i].reshape(depth, bs),
+                columns,
+                (((0,), (0,)), ((), ())),
+                preferred_element_type=F32,
+            )
+            for k in range(CHUNKS):
+                rows_k = slice(k * bs // CHUNKS, (k + 1) * bs // CHUNKS)
+                ssum[k, c, i] = part[rows_k].astype(BF16)
+
+    sums(1 - core)
 
     def sem(k, n):
         return s_sem.at[0, k, n], s_sem.at[1, k, n]
@@ -414,6 +417,7 @@
         send(ssum.at[k, 1 - core], half_recv.at[k], *sem(k, 0), (partner, y))
         for k in chunks
     ]
+    sums(core)
     after = []
     for k in chunks:
         copies[k].wait_recv()
@@ -554,7 +558,7 @@
             dma,
         ],
         compiler_params=pltpu.CompilerParams(
-            collective_id=0, has_side_effects=True, vmem_limit_bytes=64 * 2**20 - 2**17
+            collective_id=0, has_side_effects=True, vmem_limit_bytes=53 * 2**20
         ),
         name="chebyshev",
     )(block_column, block_column, ham, vec)
@@ -571,7 +575,7 @@
             pltpu.VMEM((bs, Y * bs), F32),
             dma((2, 3)),
         ],
-        compiler_params=pltpu.CompilerParams(vmem_limit_bytes=64 * 2**20 - 2**17),
+        compiler_params=pltpu.CompilerParams(vmem_limit_bytes=53 * 2**20),
         name="publish",
     )(filtered, inter)
     return filtered.reshape(24 * bs, bs), inter

time: 78.1 us -> 77.1 us (0.987)
  Pallas kernels: 77.3 us -> 75.7 us
    pallas_call x1, Pallas kernels: 75.3 us -> 73.7 us  [on_device(): pl.pallas_call(functools.partial(kernel, rows, float(rows * 24 * bs)), ou...]
where the time goes in v6:
time: 77.1 us; the launch traced here: 77 us
  Pallas kernels  75.7 us (98%)
    pallas_call x1, Pallas kernels, on_device(): pl.pallas_call(functools.partial(kernel, rows, float(rows * 24 * bs)), ou...  73.7 us
    pallas_call x1, Pallas kernels, on_device(): pl.pallas_call(publish, out_shape=(jax.ShapeDtypeStruct((24, bs, bs), BF1...  2.01 us

profile of v6, /device:TPU:1, one launch (start us, length us, event | category | flops | bytes accessed | tf_op | source)
XLA Modules:
  0.0 77.0 jit_solution(4684502297970809253)
XLA Ops:
  0.6 0.0 copy-start
  0.6 0.7 copy-done
  1.3 73.7 %chebyshev.1 = (bf16[24,128,128]{2,1,0:T(8,128)(2,1)}, f32[128,512]{1,0:T(8,128)S(1)}) custom-call(s32[288]{0:T(512)S(1)} %copy-done, s32[288]{0:T(512)S(1)} %copy-done, bf16[24,12,128,128]{3,2,1,0:T(8,128)(2,1)} %bitcast.3, bf16[24,128,128]{2,1,0:T(8,128)(2,1)} %bitcast.4), custom_call_target="tpu_custom_call" | custom-call | tf_op jit(solution)/shard_map/chebyshev/pallas_call | solution.py:523
  75.0 2.0 %publish.1 = (bf16[24,128,128]{2,1,0:T(8,128)(2,1)}, f32[128,512]{1,0:T(8,128)}) custom-call(bf16[24,128,128]{2,1,0:T(8,128)(2,1)} %get-tuple-element.6.f_from, f32[128,512]{1,0:T(8,128)S(1)} %get-tuple-element.7.inter_from), custom_call_target="tpu_custom_call" | custom-call | tf_op jit(solution)/shard_map/publish/pallas_call | solution.py:565
Async XLA Ops:
  0.6 0.7 copy-start

commit v7 on v6

--- a/solution.py
+++ b/solution.py
@@ -16,7 +16,7 @@
 HALF = 0.8
 X = 4
 Y = 4
-PARTS = (1, 1, 3)
+PARTS = (1, 1, 2)
 MOST = max(PARTS)
 CHUNKS = 1
 
@@ -252,47 +252,26 @@
         for h in range(PARTS[0]):
             send(*vector_copy(g, h, (back_to[j], y)))
 
+    second = []
+    for j in range(3):
+        quarter_copies[j].wait_recv()
+        part = hrem.at[in_group[j], :, :, rows_of(y)]
+        second.append(
+            [
+                send(
+                    part, part, fwd_sem.at[0, j, d], fwd_sem.at[1, j, d], (r, col_at(d))
+                )
+                for d in (2, 1, 3)
+            ]
+        )
     loaded(0)
     local_rows(0, 0, 6, 2)
     loaded(1)
     local_rows(0, 6, 6, 2)
-
-    fwd = []
-    for j in range(3):
-        quarter_copies[j].wait_recv()
-        part = hrem.at[in_group[j], :, :, rows_of(y)]
-        fwd.append(
-            [
-                send(
-                    part,
-                    part,
-                    fwd_sem.at[0, j, side],
-                    fwd_sem.at[1, j, side],
-                    (r, col_at(d)),
-                )
-                for side, d in enumerate((1, -1))
-            ]
-        )
     loaded(2)
     local_rows(0, 12, 6, 2)
     loaded(3)
     local_rows(0, 18, 6, 2)
-    second = []
-    for j in range(3):
-        pair = []
-        for side, d in enumerate((1, -1)):
-            fwd[j][side].wait_recv()
-            part = hrem.at[in_group[j], :, pl.ds(side, 1), rows_of(col_at(-d))]
-            pair.append(
-                send(
-                    part,
-                    part,
-                    fwd_sem.at[0, j, 2 + side],
-                    fwd_sem.at[1, j, 2 + side],
-                    (r, col_at(d)),
-                )
-            )
-        second.append(pair)
 
     def finish(step, g, h):
         args = vector_copy if step == 0 else functools.partial(product_copy, step)

time: 77.1 us -> 77.1 us (level)
  no operation moved by 1% of the time
where the time goes in v7:
time: 77.1 us; the launch traced here: 76.9 us
  Pallas kernels  75.6 us (98%)
    pallas_call x1, Pallas kernels, on_device(): pl.pallas_call(functools.partial(kernel, rows, float(rows * 24 * bs)), ou...  73.6 us
    pallas_call x1, Pallas kernels, on_device(): pl.pallas_call(publish, out_shape=(jax.ShapeDtypeStruct((24, bs, bs), BF1...  2.01 us

profile of v7, /device:TPU:1, one launch (start us, length us, event | category | flops | bytes accessed | tf_op | source)
XLA Modules:
  0.0 76.9 jit_solution(10243330436811570771)
XLA Ops:
  0.6 0.0 copy-start
  0.6 0.7 copy-done
  1.3 73.6 %chebyshev.1 = (bf16[24,128,128]{2,1,0:T(8,128)(2,1)}, f32[128,512]{1,0:T(8,128)S(1)}) custom-call(s32[288]{0:T(512)S(1)} %copy-done, s32[288]{0:T(512)S(1)} %copy-done, bf16[24,12,128,128]{3,2,1,0:T(8,128)(2,1)} %bitcast.3, bf16[24,128,128]{2,1,0:T(8,128)(2,1)} %bitcast.4), custom_call_target="tpu_custom_call" | custom-call | tf_op jit(solution)/shard_map/chebyshev/pallas_call | solution.py:502
  74.9 2.0 %publish.1 = (bf16[24,128,128]{2,1,0:T(8,128)(2,1)}, f32[128,512]{1,0:T(8,128)}) custom-call(bf16[24,128,128]{2,1,0:T(8,128)(2,1)} %get-tuple-element.6.f_from, f32[128,512]{1,0:T(8,128)S(1)} %get-tuple-element.7.inter_from), custom_call_target="tpu_custom_call" | custom-call | tf_op jit(solution)/shard_map/publish/pallas_call | solution.py:544
Async XLA Ops:
  0.6 0.7 copy-start
